TPU v7x, 256 devices: a whole 4x4x8 slice. The times are simulated.
256 devices in a mesh: ctx: 4 (over x_lo, core), fsdp: 64 (over x_hi, y, z).
Axes of the slice: x: 4 (x_hi: 2, x_lo: 2; x = x_hi * 2 + x_lo), y: 4, z: 8, core: 2. Of those that a mesh axis runs over, the one named last changes fastest.
Arguments:
- tokens: bfloat16 [8192, 6144], P('fsdp'), may hold values from -6 to 6
- expert_ids: int32 [8192, 1], P('fsdp'), may hold values from 0 to 7; in each aligned block of 128 rows (0 to 127, 128 to 255, ...) at most 17 rows name the same one
- router_gate: float32 [8192], P('fsdp'), may hold values from 0.25 to 1
- w_gate: bfloat16 [43008, 6144], P(('fsdp', 'ctx')), may hold values from -0.078125 to 0.078125
- w_up: bfloat16 [43008, 6144], P(('fsdp', 'ctx')), may hold values from -0.078125 to 0.078125
- w_down: bfloat16 [43008, 6144], P(('fsdp', 'ctx')), may hold values from -0.078125 to 0.078125
Outputs:
- expert_out: bfloat16 [8192, 6144], P('fsdp', 'ctx')
Inputs may be any that keep to these rules, and one draw needn't show every extreme that they name: `expert_ids`: among the 128 tokens of one fsdp index no expert is chosen more than 17 times, a bound that some block reaches.
All inputs are finite; a program needn't handle non-finite values.
Results may differ from a plain program's by a relative error of at most 0.014.
Values may be sent and summed in bfloat16 or wider, within the bound.
A program may use at most 128 MiB of HBM per device.

v0:
```python
import jax
import jax.numpy as jnp
from jax import lax
from jax.sharding import PartitionSpec as P

EXPERTS = 8
SLOTS = 17


def project_rows(rows, weight_rows):
    return lax.dot_general(
        rows, weight_rows, (((1,), (1,)), ((), ())), preferred_element_type=jnp.float32
    )


def expert_rows(slot_block, w_gate, w_up, w_down):
    block_shape = slot_block.shape
    flat_rows = slot_block.reshape(-1, block_shape[-1])
    gate_part = project_rows(flat_rows, w_gate)
    up_part = project_rows(flat_rows, w_up)
    hidden = (jax.nn.silu(gate_part) * up_part).astype(jnp.bfloat16)
    partial_value = jnp.dot(hidden, w_down, preferred_element_type=jnp.float32).astype(jnp.bfloat16)
    return partial_value.reshape(block_shape)


def local(tokens, expert_ids, router_gate, w_gate, w_up, w_down):
    n_fsdp = lax.axis_size("fsdp")
    group_size = n_fsdp // EXPERTS
    dmodel = tokens.shape[1]
    expert_of = expert_ids[:, 0]
    one_hot = (expert_of[:, None] == jnp.arange(EXPERTS, dtype=jnp.int32)[None, :]).astype(
        jnp.int32
    )
    slot_rank = jnp.sum((jnp.cumsum(one_hot, axis=0) - one_hot) * one_hot, axis=1)
    target = slot_rank * EXPERTS + expert_of
    selector = (jnp.arange(SLOTS * EXPERTS, dtype=jnp.int32)[:, None] == target[None, :]).astype(
        jnp.bfloat16
    )
    packed = jnp.dot(selector, tokens, preferred_element_type=jnp.float32).astype(jnp.bfloat16)
    packed = packed.reshape(SLOTS, EXPERTS, dmodel)
    copies = jnp.repeat(packed, group_size, axis=1)
    partial_rows = expert_rows(
        lax.all_to_all(copies, "fsdp", split_axis=1, concat_axis=1, tiled=True),
        w_gate,
        w_up,
        w_down,
    )
    returned = lax.all_to_all(partial_rows, "fsdp", split_axis=1, concat_axis=1, tiled=True)
    summed = jnp.sum(
        returned.reshape(SLOTS, EXPERTS, group_size, dmodel), axis=2, dtype=jnp.float32
    )
    shares = lax.psum_scatter(summed, "ctx", scatter_dimension=2, tiled=True)
    results = shares.reshape(SLOTS * EXPERTS, shares.shape[2])
    own_rows = jnp.take(results, target, axis=0)
    return (router_gate[:, None] * own_rows).astype(jnp.bfloat16)


def solution(mesh):
    placed = (
        P("fsdp", None),
        P("fsdp", None),
        P("fsdp"),
        P(("fsdp", "ctx"), None),
        P(("fsdp", "ctx"), None),
        P(("fsdp", "ctx"), None),
    )
    return jax.shard_map(
        local, mesh=mesh, in_specs=placed, out_specs=P("fsdp", "ctx"), check_vma=False
    )
```

profile of v0, /device:TPU:6, one launch (start us, length us, event | category | flops | bytes accessed | tf_op | source)
XLA Modules:
  0.0 976.5 jit_solution(13607334139903037333)
XLA Ops:
  6.5 0.0 copy-start
  6.5 0.0 reduce-scatter.2.cloned.1.call-start
  6.5 0.9 fusion.8
  7.4 0.2 reduce_window_sum.11
  7.6 0.8 select_reduce_fusion
  8.4 0.7 multiply_add_fusion
  9.1 2.0 fusion
  11.1 1.0 copy.12
  12.1 2.4 broadcast_in_dim.18
  14.5 425.1 %all_to_all.10 = bf16[17,64,6144]{2,0,1:T(8,128)(2,1)S(1)} all-to-all(bf16[17,64,6144]{2,0,1:T(8,128)(2,1)S(1)} %bitcast.27), channel_id=1, replica_groups=mesh['ctx'=4,'fsdp'=64] {'fsdp'}, dimensions={1} | all-to-all | bytes 26738688 | tf_op jit(solution)/shard_map/all_to_all | solution.py:43
  439.6 9.4 copy.13
  449.0 7.8 fusion.11
  456.8 23.6 %convolution_convert_fusion = bf16[1088,6144]{1,0:T(8,128)(2,1)} fusion(bf16[168,6144]{1,0:T(8,128)(2,1)S(1)} %copy-done, bf16[1088,6144]{1,0:T(8,128)(2,1)} %bitcast.30, bf16[168,6144]{1,0:T(8,128)(2,1)} %param.10, f32[1088,168]{0,1:T(8,128)S(1)} %fusion.11), kind=kOutput, calls=%fused_computation.2 | convolution fusion | flops 4499880960 | bytes 31598592 | tf_op jit(solution)/shard_map/dot_general | solution.py:22
  480.4 12.1 %copy.14 = bf16[17,64,6144]{2,0,1:T(8,128)(2,1)S(1)} copy(bf16[17,64,6144]{2,1,0:T(8,128)(2,1)} %bitcast.31) | data formatting | bytes 26738688 | tf_op jit(solution)/shard_map/reshape | solution.py:23
  492.5 417.7 %all_to_all.11 = bf16[17,64,6144]{2,0,1:T(8,128)(2,1)S(1)} all-to-all(bf16[17,64,6144]{2,0,1:T(8,128)(2,1)S(1)} %copy.14), channel_id=1, replica_groups=mesh['ctx'=4,'fsdp'=64] {'fsdp'}, dimensions={1} | all-to-all | bytes 26738688 | tf_op jit(solution)/shard_map/all_to_all | solution.py:48
  910.2 6.5 convert_reduce_fusion
  916.7 0.0 reduce-scatter.2.cloned.1.call-update
  916.7 0.6 copy-done.2
  917.4 46.8 %reduce-scatter.2.cloned.1.call-done = f32[17,8,1536]{2,0,1:T(8,128)} async-done(((f32[17,8,6144]{2,0,1:T(8,128)}), f32[17,8,1536]{2,0,1:T(8,128)}) %reduce-scatter.2.cloned.1.call-update) | async-done | bytes 835600 | tf_op jit(solution)/shard_map/reduce_scatter | solution.py:52
  964.1 1.8 copy.17
  965.9 0.0 copy-start.3
  965.9 0.0 copy-start.1
  965.9 1.7 gather_fusion
  967.6 2.0 multiply_convert_fusion
  (8 shorter events, 0.0 us)
Async XLA Ops:
  6.5 450.3 %copy-start = (bf16[168,6144]{1,0:T(8,128)(2,1)S(1)}, bf16[168,6144]{1,0:T(8,128)(2,1)}, u32[]{:S(2)}) copy-start(bf16[168,6144]{1,0:T(8,128)(2,1)} %param.11) | copy-start | bytes 6193156
  6.5 957.6 %reduce-scatter.2.cloned.1.call-start = ((), (), s32[]{:S(2)}) async-start(), calls=%async_computation.3 | async-start | bytes 5898240 | tf_op jit(solution)/shard_map/reduce_scatter | solution.py:52
  439.6 9.4 copy-start.4
  916.7 0.7 copy-start.2
  965.9 1.8 copy-start.3
  965.9 3.8 copy-start.1
Sparse Core Ops, SparseCore 0:
  916.8 47.2 reduce-scatter.1
where the time goes:
time: 979 us; the launch traced here: 977 us
  blocking collectives  843 us (86%)
  waiting for transfers between devices  46.8 us (5%)
  matrix products  33.4 us (3%)
  local copies, waits for them, and re-layouts  29 us (3%)
  between operations  13.5 us (1%)
  other arithmetic  11.1 us (1%)
    all_to_all x1, blocking collectives, local(): lax.all_to_all(copies, 'fsdp', split_axis=1, concat_axis=1, tiled=True)  425 us
    all_to_all x1, blocking collectives, local(): lax.all_to_all(partial_rows, 'fsdp', split_axis=1, concat_axis=1, tiled=T...  418 us
    reduce_scatter x1, waiting for transfers between devices, local(): shares = lax.psum_scatter(summed, 'ctx', scatter_dimension=2, tiled=True)  46.8 us
    dot_general x1, matrix products, expert_rows(): jnp.dot(hidden, w_down, preferred_element_type=jnp.float32)  23.6 us
  transfers between devices with their start and end apart: 1, of which 1 were waited for; matrix products, arithmetic and copies ran while one was open for 0% of the time, Pallas kernels for 0%

commit v1 on v0

v1 whole, which is shorter than its diff:
```python
import functools

import jax
import jax.numpy as jnp
from jax import lax
from jax.experimental import pallas as pl
from jax.experimental.pallas import tpu as pltpu
from jax.sharding import PartitionSpec as P

MESH = pl.DeviceIdType.MESH
EXPERTS = 8
MAIN = 16
PAIR = 32
ROWS = EXPERTS * MAIN + MAIN
RING = 8
HALF = ((0, 80), (80, 64))
BF16, F32 = jnp.bfloat16, jnp.float32


def nt_dot(a, b):
    return lax.dot_general(a, b, (((1,), (1,)), ((), ())), preferred_element_type=F32)


def kernel(
    tok_ref, ids_ref, gate_ref, wg_ref, wu_ref, wd_ref,
    out_ref,
    sel, send, staged, x, wgu, wdn, gu_own, gu_out, gu_in, hid, y, yx, back, final, fx, parcel, result,
    w_sem, ws_sem, wr_sem, as_sem, ar_sem, zs_sem, zr_sem, xs_sem, xr_sem,
    gs_sem, gr_sem, hs_sem, hr_sem, ys_sem, yr_sem, bs_sem, br_sem, fs_sem, fr_sem, ds_sem, dr_sem,
):
    c, f = lax.axis_index("ctx"), lax.axis_index("fsdp")
    xl, co = c // 2, c % 2
    col, z = f // RING, f % RING
    units = wg_ref.shape[0]
    width = x.shape[3]

    def on_z(d):
        return (c, col * RING + (z + d + RING) % RING)

    def in_column(e):
        return (c, e * RING + z)

    sibling = (c + 1 - 2 * co, f)
    across = ((c + 2) % 4, f)

    def remote(src, dst, ssem, rsem, dev):
        return pltpu.make_async_remote_copy(
            src_ref=src, dst_ref=dst, send_sem=ssem, recv_sem=rsem, device_id=dev, device_id_type=MESH
        )

    barrier = pltpu.get_barrier_semaphore()
    partners = [on_z(1), on_z(-1), sibling, across] + [in_column((col + i) % EXPERTS) for i in range(1, EXPERTS)]
    for dev in partners:
        pl.semaphore_signal(barrier, inc=1, device_id=dev, device_id_type=MESH)

    def column_of(core, blk):
        return pl.multiple_of(((blk % 2) * 2 + core) * 2 * width + (blk // 2) * width, 128)

    def weight_slot(m, unit_core, blk):
        return wdn.at[unit_core, blk] if m == 2 else wgu.at[m, unit_core, blk]

    w_refs = (wg_ref, wu_ref, wd_ref)
    own_w = [
        pltpu.make_async_copy(
            w_refs[m].at[:, pl.ds(column_of(co, blk), width)], weight_slot(m, co, blk), w_sem.at[m, blk]
        )
        for m in range(3) for blk in range(4)
    ]
    other_w = [
        remote(
            w_refs[m].at[:, pl.ds(column_of(1 - co, blk), width)], weight_slot(m, co, blk),
            ws_sem.at[m, blk], wr_sem.at[m, blk], sibling,
        )
        for m in range(3) for blk in range(4)
    ]
    for cp in own_w:
        cp.start()

    n_tok = tok_ref.shape[0]
    rows_i = lax.broadcasted_iota(jnp.int32, (n_tok, n_tok), 0)
    cols_i = lax.broadcasted_iota(jnp.int32, (n_tok, n_tok), 1)
    ids_row = ids_ref[...]
    ids_col = jnp.sum(jnp.where(rows_i == cols_i, ids_row, 0), axis=1, keepdims=True)
    gate_col = jnp.sum(jnp.where(rows_i == cols_i, gate_ref[...], 0.0), axis=1, keepdims=True)
    same = (ids_row == ids_col) & (cols_i < rows_i)
    rank = jnp.sum(same.astype(jnp.int32), axis=1, keepdims=True)
    place = ids_col * PAIR + jnp.where(rank < MAIN, rank, MAIN + col)
    slots = lax.broadcasted_iota(jnp.int32, (n_tok, EXPERTS * PAIR), 1)
    select = (slots == place).astype(F32)
    sel[...] = select.astype(BF16)
    pack = jnp.transpose(select).astype(BF16)
    share_cols = (column_of(co, 0), column_of(co, 1), column_of(co, 2 + xl))
    for p in range(3):
        packed = jnp.dot(pack, tok_ref[:, pl.ds(share_cols[p], width)], preferred_element_type=F32)
        send[:, :, p * width:(p + 1) * width] = packed.astype(BF16).reshape(EXPERTS, PAIR, width)

    pl.semaphore_wait(barrier, len(partners))

    def phase_a(i):
        return remote(
            send.at[(col + i) % EXPERTS], staged.at[col], as_sem.at[i - 1], ar_sem.at[i - 1],
            in_column((col + i) % EXPERTS),
        )

    to_experts = [phase_a(i) for i in range(1, EXPERTS)]
    for cp in to_experts:
        cp.start()
    for cp in other_w:
        cp.start()
    staged[col] = send[col]
    for cp in to_experts:
        cp.wait()

    def piece_of(p):
        return 2 + xl if p == 2 else p

    for p in range(3):
        cs = slice(p * width, (p + 1) * width)
        extra = staged[0, MAIN:, cs]
        for s in range(EXPERTS):
            x[z, piece_of(p), s * MAIN:(s + 1) * MAIN, :] = staged[s, :MAIN, cs]
            if s:
                extra = extra + staged[s, MAIN:, cs]
        x[z, piece_of(p), EXPERTS * MAIN:, :] = extra

    def plane(d):
        return (z + d + RING) % RING

    def z_send(side, k, p):
        d = 1 - 2 * side
        blk = x.at[plane(-d * (k - 1)), piece_of(p)]
        if k == 4:
            blk = blk.at[pl.ds(*HALF[side])]
        return remote(blk, blk, zs_sem.at[side, k - 1, p], zr_sem.at[side, k - 1, p], on_z(d))

    def x_send(i):
        side, k = (i + 1) % 2, (i + 1) // 2
        if i == 0:
            blk = x.at[z, 2 + xl]
        elif i < 7:
            blk = x.at[plane(-(1 - 2 * side) * k), 2 + xl]
        else:
            side = i - 7
            blk = x.at[plane(4), 2 + xl].at[pl.ds(*HALF[side])]
        return remote(blk, blk, xs_sem.at[i], xr_sem.at[i], across)

    order = [0, -1, 1, -2, 2, -3, 3, 4]

    def gu_send(i):
        return remote(gu_out.at[i], gu_in.at[i], gs_sem.at[i], gr_sem.at[i], sibling)

    def hid_send(i):
        return remote(hid.at[i, co], hid.at[i, co], hs_sem.at[i], hr_sem.at[i], sibling)

    def gate_up(i):
        pi = plane(order[i])
        x_send(i).wait_recv()
        if i == 7:
            x_send(8).wait_recv()
        for m in range(2):
            gu_own[i, m] = jnp.zeros(gu_own.shape[2:], F32)
            gu_out[i, m] = jnp.zeros(gu_own.shape[2:], F32)

        def body(blk, carry):
            xb = x[pi, blk]
            for m in range(2):
                gu_own[i, m] += nt_dot(xb, wgu[m, co, blk])
                gu_out[i, m] += nt_dot(xb, wgu[m, 1 - co, blk])
            return carry

        lax.fori_loop(0, 4, body, 0)
        gu_send(i).start()

    def hidden(i):
        gu_send(i).wait_recv()
        g = gu_own[i, 0] + gu_in[i, 0]
        u = gu_own[i, 1] + gu_in[i, 1]
        hid[i, co] = (g / (1.0 + jnp.exp(-g)) * u).astype(BF16)
        hid_send(i).start()

    def y_send(i):
        return remote(y.at[plane(order[i]), 2 + 1 - xl], yx.at[i], ys_sem.at[i], yr_sem.at[i], across)

    def down(i):
        pi = plane(order[i])
        hid_send(i).wait_recv()

        def body(blk, carry):
            part = jnp.dot(hid[i, 0], wdn[0, blk], preferred_element_type=F32)
            part += jnp.dot(hid[i, 1], wdn[1, blk], preferred_element_type=F32)
            y[pi, blk] = part.astype(BF16)
            return carry

        lax.fori_loop(0, 4, body, 0)
        y_send(i).start()

    def add_across(i):
        y_send(i).wait()
        pi = plane(order[i])
        y[pi, 2 + xl] = (y[pi, 2 + xl].astype(F32) + yx[i].astype(F32)).astype(BF16)

    def compute(i):
        if i < 8:
            gate_up(i)
        if 0 < i < 9:
            hidden(i - 1)
        if 1 < i:
            down(i - 2)

    pieces = (2, 0, 1)
    x_send(0).start()
    for p in pieces:
        for side in range(2):
            z_send(side, 1, p).start()
    for cp in own_w:
        cp.wait()
    for cp in other_w:
        cp.wait()
    compute(0)
    for k in range(2, 5):
        for p in pieces:
            for side in range(2):
                z_send(side, k - 1, p).wait_recv()
                z_send(side, k, p).start()
                if p == 2:
                    x_send(2 * (k - 1) - 1 + side).start()
        compute(2 * (k - 1) - 1)
        compute(2 * (k - 1))
    for p in pieces:
        for side in range(2):
            z_send(side, 4, p).wait_recv()
            if p == 2:
                x_send(7 + side).start()
    for i in range(7, 10):
        compute(i)

    def back_send(side, j, p):
        d = 1 - 2 * side
        src = y.at[plane(d * (5 - j)), piece_of(p)]
        dst = back.at[side, j - 1, p]
        if j == 1:
            src, dst = src.at[pl.ds(*HALF[side])], dst.at[pl.ds(*HALF[side])]
        return remote(src, dst, bs_sem.at[side, j - 1, p], br_sem.at[side, j - 1, p], on_z(d))

    def index_of(d):
        return order.index(d)

    for j in range(1, 5):
        for p in (0, 1, 2):
            for side in range(2):
                d = 1 - 2 * side
                if p == 2 and (j > 1 or side == 0):
                    add_across(7 if j == 1 else index_of(d * (5 - j)))
                if j > 1:
                    back_send(side, j - 1, p).wait_recv()
                    pi = plane(d * (5 - j))
                    rows = pl.ds(*HALF[side]) if j == 2 else slice(None)
                    y[pi, piece_of(p), rows, :] = (
                        y[pi, piece_of(p), rows, :].astype(F32) + back[side, j - 2, p, rows, :].astype(F32)
                    ).astype(BF16)
                back_send(side, j, p).start()
    add_across(0)
    f_send = remote(final.at[1 - xl], fx, fs_sem, fr_sem, across)
    for p in range(3):
        for side in range(2):
            back_send(side, 4, p).wait_recv()
        total = y[z, piece_of(p)].astype(F32) + back[0, 3, p].astype(F32) + back[1, 3, p].astype(F32)
        final[p] = total.astype(BF16)
        if p == 1:
            f_send.start()
    f_send.wait()
    mine = (final[xl].astype(F32) + fx[...].astype(F32)).astype(BF16)
    rest = final[2]
    for s in range(EXPERTS):
        parcel[s, :MAIN, :width] = mine[s * MAIN:(s + 1) * MAIN]
        parcel[s, :MAIN, width:] = rest[s * MAIN:(s + 1) * MAIN]
        parcel[s, MAIN:, :width] = mine[EXPERTS * MAIN:]
        parcel[s, MAIN:, width:] = rest[EXPERTS * MAIN:]

    def deliver(i):
        return remote(
            parcel.at[(col + i) % EXPERTS], result.at[col], ds_sem.at[i - 1], dr_sem.at[i - 1],
            in_column((col + i) % EXPERTS),
        )

    to_owners = [deliver(i) for i in range(1, EXPERTS)]
    for cp in to_owners:
        cp.start()
    result[col] = parcel[col]

    x_sends = [x_send(i) for i in range(9)]
    for cp in x_sends:
        cp.wait_send()
    for i in range(8):
        gu_send(i).wait_send()
        hid_send(i).wait_send()
    for side in range(2):
        for k in range(1, 5):
            for p in range(3):
                z_send(side, k, p).wait_send()
                back_send(side, k, p).wait_send()
    for cp in to_owners:
        cp.wait()
    rows = jnp.dot(sel[...], result[...].reshape(EXPERTS * PAIR, 2 * width), preferred_element_type=F32)
    out_ref[...] = (gate_col * rows).astype(BF16)


def local(tokens, expert_ids, router_gate, w_gate, w_up, w_down):
    n_tok, dmodel = tokens.shape
    units = w_gate.shape[0]
    width = dmodel // 8
    vmem, dma = pltpu.VMEM, pltpu.SemaphoreType.DMA
    return pl.pallas_call(
        kernel,
        out_shape=jax.ShapeDtypeStruct((n_tok, 2 * width), BF16),
        in_specs=[pl.BlockSpec(memory_space=pltpu.VMEM)] * 3 + [pl.BlockSpec(memory_space=pl.ANY)] * 3,
        out_specs=pl.BlockSpec(memory_space=pltpu.VMEM),
        scratch_shapes=[
            vmem((n_tok, EXPERTS * PAIR), BF16),
            vmem((EXPERTS, PAIR, 3 * width), BF16),
            vmem((EXPERTS, PAIR, 3 * width), BF16),
            vmem((RING, 4, ROWS, width), BF16),
            vmem((2, 2, 4, units, width), BF16),
            vmem((2, 4, units, width), BF16),
            vmem((RING, 2, ROWS, units), F32),
            vmem((RING, 2, ROWS, units), F32),
            vmem((RING, 2, ROWS, units), F32),
            vmem((RING, 2, ROWS, units), BF16),
            vmem((RING, 4, ROWS, width), BF16),
            vmem((RING, ROWS, width), BF16),
            vmem((2, 4, 3, ROWS, width), BF16),
            vmem((3, ROWS, width), BF16),
            vmem((ROWS, width), BF16),
            vmem((EXPERTS, PAIR, 2 * width), BF16),
            vmem((EXPERTS, PAIR, 2 * width), BF16),
            dma((3, 4)), dma((3, 4)), dma((3, 4)),
            dma((7,)), dma((7,)),
            dma((2, 4, 3)), dma((2, 4, 3)),
            dma((9,)), dma((9,)),
            dma((8,)), dma((8,)),
            dma((8,)), dma((8,)),
            dma((8,)), dma((8,)),
            dma((2, 4, 3)), dma((2, 4, 3)),
            dma, dma,
            dma((7,)), dma((7,)),
        ],
        compiler_params=pltpu.CompilerParams(
            collective_id=0, has_side_effects=True, vmem_limit_bytes=60 * 2**20
        ),
        cost_estimate=pl.CostEstimate(flops=7 * 10**9, bytes_accessed=10**7, transcendentals=200000),
        name="routed_experts",
    )(tokens, expert_ids.reshape(1, n_tok), router_gate.reshape(1, n_tok), w_gate, w_up, w_down)


def solution(mesh):
    placed = (
        P("fsdp", None),
        P("fsdp", None),
        P("fsdp"),
        P(("fsdp", "ctx"), None),
        P(("fsdp", "ctx"), None),
        P(("fsdp", "ctx"), None),
    )
    return jax.shard_map(
        local, mesh=mesh, in_specs=placed, out_specs=P("fsdp", "ctx"), check_vma=False
    )
```

time: 979 us -> 181 us (0.18)
  blocking collectives: 843 us -> 0 us
  Pallas kernels: 0 us -> 178 us
  waiting for transfers between devices: 46.8 us -> 0 us
  matrix products: 33.4 us -> 0 us
  local copies, waits for them, and re-layouts: 29 us -> 1.77 us
  between operations: 13.5 us -> 0.01 us
  other arithmetic: 11.1 us -> 0 us
    all_to_all x2 -> x0, blocking collectives: 843 us -> none  [the longest x1 425 us: local(): lax.all_to_all(copies, 'fsdp', split_axis=1, concat_axis=1, tiled=True)]
    pallas_call x0 -> x1, Pallas kernels: none -> 178 us  [local(): pl.pallas_call(kernel, out_shape=jax.ShapeDtypeStruct((n_tok, 2 * width),...]
    reduce_scatter x1 -> x0, waiting for transfers between devices: 46.8 us -> none  [local(): shares = lax.psum_scatter(summed, 'ctx', scatter_dimension=2, tiled=True)]
    dot_general x3 -> x0, matrix products: 33.4 us -> none  [the longest x1 23.6 us: expert_rows(): jnp.dot(hidden, w_down, preferred_element_type=jnp.float32)]
    reshape x2 -> x0, local copies, waits for them, and re-layouts: 13.1 us -> none  [the longest x1 12.1 us: expert_rows(): return partial_value.reshape(block_shape)]
  transfers between devices with their start and end apart: 1 -> 0, of which waited for: 1 -> 0; matrix products, arithmetic and copies ran while one was open for 0% -> 0% of each run, Pallas kernels for 0% -> 0%
where the time goes in v1:
time: 181 us; the launch traced here: 180 us
  Pallas kernels  178 us (98%)
    pallas_call x1, Pallas kernels, local(): pl.pallas_call(kernel, out_shape=jax.ShapeDtypeStruct((n_tok, 2 * width),...  178 us

profile of v1, /device:TPU:6, one launch (start us, length us, event | category | flops | bytes accessed | tf_op | source)
XLA Modules:
  0.0 179.7 jit_solution(17826135883904241273)
XLA Ops:
  0.0 177.9 %routed_experts.1 = bf16[128,1536]{1,0:T(8,128)(2,1)} custom-call(bf16[128,6144]{1,0:T(8,128)(2,1)} %tok_ref.1, s32[1,128]{1,0:T(1,128)} %bitcast.2, f32[1,128]{1,0:T(1,128)} %bitcast.3, bf16[168,6144]{1,0:T(8,128)(2,1)} %wg_ref.1, bf16[168,6144]{1,0:T(8,128)(2,1)} %wu_ref.1, bf16[168,6144]{1,0:T(8,128)(2,1)} %wd_ref.1), custom_call_target="tpu_custom_call" | custom-call | flops 7000000000 | bytes 10000000 | tf_op jit(solution)/shard_map/routed_experts/pallas_call | solution.py:313
  177.9 1.8 copy.8

commit v2 on v0

v2 whole, which is shorter than its diff:
```python
import functools

import jax
import jax.numpy as jnp
from jax import lax
from jax.experimental import pallas as pl
from jax.experimental.pallas import tpu as pltpu
from jax.sharding import PartitionSpec as P

MESH = pl.DeviceIdType.MESH
EXPERTS = 8
MAIN = 16
RING = 8
BF16, F32 = jnp.bfloat16, jnp.float32
SOURCES = ((0, 0), (0, 2), (1, 0), (1, 2), (0, 1), (0, 3), (1, 1), (1, 3))
ROWS = (4 * MAIN, 5 * MAIN)
HALF = (((0, 32), (32, 32)), ((0, 48), (48, 32)))
ORDER = (0, -1, 1, -2, 2, -3, 3, 4)
GROUPS = ((0, 3), (3, 5), (5, 7), (7, 8))


def nt_dot(a, b):
    return lax.dot_general(a, b, (((1,), (1,)), ((), ())), preferred_element_type=F32)


def dot(a, b):
    return jnp.dot(a, b, preferred_element_type=F32)


def transposition(shape):
    r = lax.broadcasted_iota(jnp.int32, shape, 0)
    q = lax.broadcasted_iota(jnp.int32, shape, 1)
    return (((r >> 4) == (q & 15)) & ((r & 15) == (q >> 4))).astype(F32).astype(BF16)


def fold(rows):
    tiles = []
    for lo in range(0, rows.shape[1], 2048):
        part = rows[:, lo:lo + 2048]
        n = part.shape[1] // 128
        stack = jnp.concatenate([part[:, j * 128:(j + 1) * 128] for j in range(n)], axis=0)
        tiles.append(dot(transposition((128, n * 16)), stack).astype(BF16))
    return tiles


def unfold(tiles, n_blocks):
    blocks = []
    for t, tile in enumerate(tiles):
        n = min(16, n_blocks - 16 * t)
        stack = dot(transposition((n * 16, 128)), tile).astype(BF16)
        blocks += [stack[j * 16:(j + 1) * 16] for j in range(n)]
    return jnp.concatenate(blocks, axis=1)


def kernel(
    tok_ref, ids_ref, gate_ref, wg_ref, wu_ref, wd_ref,
    out_ref,
    sel, send, staged, wgu, wdn, parcel, parcel_x, result, result_x, *rest,
):
    per_wave, sems = rest[:20], rest[20:]
    x, gu_own, gu_out, gu_in, hid, y, yx, back, final, fx = [per_wave[2 * i:2 * i + 2] for i in range(10)]
    (
        w_sem, ws_sem, wr_sem, as_sem, ar_sem, zs_sem, zr_sem, xs_sem, xr_sem,
        gs_sem, gr_sem, hs_sem, hr_sem, ys_sem, yr_sem, bs_sem, br_sem, fs_sem, fr_sem,
        ds_sem, dr_sem, es_sem, er_sem,
    ) = sems
    c, f = lax.axis_index("ctx"), lax.axis_index("fsdp")
    xl, co = c // 2, c % 2
    col, z = f // RING, f % RING
    width = x[0].shape[3]
    share = 3 * width

    def on_z(d):
        return (c, col * RING + (z + d + RING) % RING)

    def column(r, sign):
        dx, dy = SOURCES[r]
        return (col // 4 + dx) % 2 * 4 + (col % 4 + sign * dy + 4) % 4

    def in_column(e):
        return (c, e * RING + z)

    sibling = (c + 1 - 2 * co, f)
    across = ((c + 2) % 4, f)

    def remote(src, dst, ssem, rsem, dev):
        return pltpu.make_async_remote_copy(
            src_ref=src, dst_ref=dst, send_sem=ssem, recv_sem=rsem, device_id=dev, device_id_type=MESH
        )

    barrier = pltpu.get_barrier_semaphore()
    partners = [on_z(1), on_z(-1), sibling, across] + [in_column((col + i) % EXPERTS) for i in range(1, EXPERTS)]
    for dev in partners:
        pl.semaphore_signal(barrier, inc=1, device_id=dev, device_id_type=MESH)

    def column_of(core, blk):
        return pl.multiple_of(((blk % 2) * 2 + core) * 2 * width + (blk // 2) * width, 128)

    def weight_slot(m, unit_core, blk):
        return wdn.at[unit_core, blk] if m == 2 else wgu.at[m, unit_core, blk]

    w_refs = (wg_ref, wu_ref, wd_ref)
    own_w = [
        pltpu.make_async_copy(
            w_refs[m].at[:, pl.ds(column_of(co, blk), width)], weight_slot(m, co, blk), w_sem.at[m, blk]
        )
        for m in range(3) for blk in range(4)
    ]
    other_w = [
        remote(
            w_refs[m].at[:, pl.ds(column_of(1 - co, blk), width)], weight_slot(m, co, blk),
            ws_sem.at[m, blk], wr_sem.at[m, blk], sibling,
        )
        for m in range(3) for blk in range(4)
    ]
    for cp in own_w:
        cp.start()

    n_tok = tok_ref.shape[0]
    rows_i = lax.broadcasted_iota(jnp.int32, (n_tok, n_tok), 0)
    cols_i = lax.broadcasted_iota(jnp.int32, (n_tok, n_tok), 1)
    ids_row = ids_ref[...]
    ids_col = jnp.sum(jnp.where(rows_i == cols_i, ids_row, 0), axis=1, keepdims=True)
    gate_col = jnp.sum(jnp.where(rows_i == cols_i, gate_ref[...], 0.0), axis=1, keepdims=True)
    same = (ids_row == ids_col) & (cols_i < rows_i)
    rank = jnp.sum(same.astype(jnp.int32), axis=1, keepdims=True)
    main = ((cols_i == ids_col * MAIN + rank) & (rank < MAIN)).astype(F32)
    last = ((cols_i == ids_col) & (rank == MAIN)).astype(F32)
    sel[0] = main.astype(BF16)
    sel[1] = last.astype(BF16)
    pack = jnp.transpose(main).astype(BF16)
    pack_last = jnp.transpose(last)[:16].astype(BF16)
    share_cols = (column_of(co, 0), column_of(co, 1), column_of(co, 2 + xl))
    lasts = []
    for p in range(3):
        part = tok_ref[:, pl.ds(share_cols[p], width)]
        send[:, :, p * width:(p + 1) * width] = dot(pack, part).astype(BF16).reshape(EXPERTS, MAIN, width)
        lasts.append(dot(pack_last, part).astype(BF16))
    for t, tile in enumerate(fold(jnp.concatenate(lasts, axis=1))):
        send[:, :, share + t * 128:share + (t + 1) * 128] = tile.reshape(EXPERTS, MAIN, 128)

    pl.semaphore_wait(barrier, len(partners))

    def phase_a(r):
        e = column(r, -1)
        return remote(send.at[e], staged.at[r], as_sem.at[r], ar_sem.at[r], in_column(e))

    def piece_of(p):
        return 2 + xl if p == 2 else p

    def land(w):
        for q in range(4):
            r = 4 * w + q
            if r == 0:
                staged[0] = send[col]
            else:
                phase_a(r).wait_recv()
            for p in range(3):
                x[w][z, piece_of(p), q * MAIN:(q + 1) * MAIN, :] = staged[r, :, p * width:(p + 1) * width]
        if w == 1:
            tiles = [
                staged[:, :, lo:lo + 128].reshape(EXPERTS * MAIN, 128)
                for lo in range(share, staged.shape[2], 128)
            ]
            extra = unfold(tiles, share // 128)
            for p in range(3):
                x[1][z, piece_of(p), 4 * MAIN:, :] = extra[:, p * width:(p + 1) * width]

    def plane(d):
        return (z + d + RING) % RING

    def z_send(w, side, k, p):
        d = 1 - 2 * side
        blk = x[w].at[plane(-d * (k - 1)), piece_of(p)]
        if k == 4:
            blk = blk.at[pl.ds(*HALF[w][side])]
        return remote(blk, blk, zs_sem.at[w, side, k - 1, p], zr_sem.at[w, side, k - 1, p], on_z(d))

    def x_send(w, i):
        if i < 7:
            blk = x[w].at[plane(ORDER[i]), 2 + xl]
        else:
            blk = x[w].at[plane(4), 2 + xl].at[pl.ds(*HALF[w][i - 7])]
        return remote(blk, blk, xs_sem.at[w, i], xr_sem.at[w, i], across)

    def z_step(w, k):
        for p in (2, 0, 1):
            for side in range(2):
                if k > 1:
                    z_send(w, side, k - 1, p).wait_recv()
                if k < 5:
                    z_send(w, side, k, p).start()
                if p == 2 and k > 1:
                    x_send(w, 2 * (k - 1) - 1 + side).start()
                elif p == 2 and side == 0:
                    x_send(w, 0).start()

    def group_rows(w, g):
        return GROUPS[g][0] * ROWS[w], (GROUPS[g][1] - GROUPS[g][0]) * ROWS[w]

    def gu_send(w, g):
        rows = pl.ds(*group_rows(w, g))
        return remote(gu_out[w].at[:, rows], gu_in[w].at[:, rows], gs_sem.at[w, g], gr_sem.at[w, g], sibling)

    def hid_send(w, g):
        mine = hid[w].at[co, pl.ds(*group_rows(w, g))]
        return remote(mine, mine, hs_sem.at[w, g], hr_sem.at[w, g], sibling)

    def gate_up(w, g):
        lo, n = group_rows(w, g)
        ids = range(*GROUPS[g])
        for i in ids:
            x_send(w, i).wait_recv()
            if i == 7:
                x_send(w, 8).wait_recv()
        for m in range(2):
            gu_own[w][m, lo:lo + n] = jnp.zeros((n, gu_own[w].shape[2]), F32)
            gu_out[w][m, lo:lo + n] = jnp.zeros((n, gu_own[w].shape[2]), F32)

        def body(blk, carry):
            xb = jnp.concatenate([x[w][plane(ORDER[i]), blk] for i in ids], axis=0)
            for m in range(2):
                gu_own[w][m, lo:lo + n] += nt_dot(xb, wgu[m, co, blk])
                gu_out[w][m, lo:lo + n] += nt_dot(xb, wgu[m, 1 - co, blk])
            return carry

        lax.fori_loop(0, 4, body, 0)
        gu_send(w, g).start()

    def hidden(w, g):
        lo, n = group_rows(w, g)
        gu_send(w, g).wait_recv()
        gate = gu_own[w][0, lo:lo + n] + gu_in[w][0, lo:lo + n]
        up = gu_own[w][1, lo:lo + n] + gu_in[w][1, lo:lo + n]
        hid[w][co, lo:lo + n] = (gate / (1.0 + jnp.exp(-gate)) * up).astype(BF16)
        hid_send(w, g).start()

    def down(w, g):
        lo, n = group_rows(w, g)
        hid_send(w, g).wait_recv()

        def body(blk, carry):
            part = dot(hid[w][0, lo:lo + n], wdn[0, blk]) + dot(hid[w][1, lo:lo + n], wdn[1, blk])
            part = part.astype(BF16)
            for at, i in enumerate(range(*GROUPS[g])):
                y[w][plane(ORDER[i]), blk] = part[at * ROWS[w]:(at + 1) * ROWS[w]]
            return carry

        lax.fori_loop(0, 4, body, 0)

    def y_send(w, i):
        return remote(
            y[w].at[plane(ORDER[i]), 2 + 1 - xl], yx[w].at[i], ys_sem.at[w, i], yr_sem.at[w, i], across
        )

    def add_across(w, i):
        y_send(w, i).wait()
        pi = plane(ORDER[i])
        y[w][pi, 2 + xl] = (y[w][pi, 2 + xl].astype(F32) + yx[w][i].astype(F32)).astype(BF16)

    def back_send(w, side, j, p):
        d = 1 - 2 * side
        src = y[w].at[plane(d * (5 - j)), piece_of(p)]
        dst = back[w].at[side, j - 1, p]
        if j == 1:
            src, dst = src.at[pl.ds(*HALF[w][side])], dst.at[pl.ds(*HALF[w][side])]
        return remote(src, dst, bs_sem.at[w, side, j - 1, p], br_sem.at[w, side, j - 1, p], on_z(d))

    def ret(w, j, *ps):
        for p in ps:
            for side in range(2):
                d = 1 - 2 * side
                far = plane(d * (5 - j))
                if p == 2 and (j > 1 or side == 0):
                    add_across(w, ORDER.index(d * (5 - j)))
                if j > 1:
                    back_send(w, side, j - 1, p).wait_recv()
                    lo, n = HALF[w][side] if j == 2 else (0, ROWS[w])
                    y[w][far, piece_of(p), lo:lo + n, :] = (
                        y[w][far, piece_of(p), lo:lo + n, :].astype(F32)
                        + back[w][side, j - 2, p, lo:lo + n, :].astype(F32)
                    ).astype(BF16)
                back_send(w, side, j, p).start()

    def f_send(w):
        return remote(final[w].at[1 - xl], fx[w], fs_sem.at[w], fr_sem.at[w], across)

    def finish(w, *ps):
        for p in ps:
            if p == 2:
                add_across(w, 0)
            for side in range(2):
                back_send(w, side, 4, p).wait_recv()
            total = y[w][z, piece_of(p)].astype(F32) + back[w][0, 3, p].astype(F32) + back[w][1, 3, p].astype(F32)
            final[w][p] = total.astype(BF16)
            if p == 1:
                f_send(w).start()

    def deliver(r):
        s = column(r, 1)
        return remote(parcel.at[r], result.at[col], ds_sem.at[r], dr_sem.at[r], in_column(s))

    def deliver_last(r):
        s = column(r, 1)
        return remote(parcel_x.at[r], result_x.at[col], es_sem.at[r], er_sem.at[r], in_column(s))

    def hand_out(w):
        f_send(w).wait()
        mine = (final[w][xl].astype(F32) + fx[w][...].astype(F32)).astype(BF16)
        rest_of = final[w][2]
        for q in range(4):
            r = 4 * w + q
            parcel[r, :, :width] = mine[q * MAIN:(q + 1) * MAIN]
            parcel[r, :, width:] = rest_of[q * MAIN:(q + 1) * MAIN]
            if r:
                deliver(r).start()
            else:
                result[col] = parcel[0]
        if w == 1:
            tile = fold(jnp.concatenate([mine[4 * MAIN:], rest_of[4 * MAIN:]], axis=1))[0]
            parcel_x[...] = tile.reshape(EXPERTS, MAIN, 128)
            result_x[col] = parcel_x[0]
            for r in range(1, EXPERTS):
                deliver_last(r).start()

    for r in range(1, EXPERTS):
        phase_a(r).start()
    for cp in other_w:
        cp.start()

    def cross(w, *idx):
        for i in idx:
            y_send(w, i).start()

    land(0)
    z_step(0, 1)
    land(1)
    for cp in own_w + other_w:
        cp.wait()
    z_step(0, 2)
    gate_up(0, 0)
    z_step(0, 3)
    gate_up(0, 1)
    hidden(0, 0)
    z_step(0, 4)
    z_step(1, 1)
    gate_up(0, 2)
    hidden(0, 1)
    down(0, 0)
    z_step(0, 5)
    z_step(1, 2)
    hidden(0, 2)
    gate_up(0, 3)
    down(0, 1)
    down(0, 2)
    cross(0, 5, 6)
    hidden(0, 3)
    down(0, 3)
    cross(0, 7)
    ret(0, 1, 0, 1)
    z_step(1, 3)
    cross(0, 3, 4)
    gate_up(1, 0)
    ret(0, 2, 0, 1)
    ret(0, 1, 2)
    z_step(1, 4)
    cross(0, 1, 2)
    gate_up(1, 1)
    hidden(1, 0)
    ret(0, 3, 0, 1)
    ret(0, 2, 2)
    z_step(1, 5)
    cross(0, 0)
    gate_up(1, 2)
    hidden(1, 1)
    down(1, 0)
    ret(0, 4, 0, 1)
    ret(0, 3, 2)
    gate_up(1, 3)
    hidden(1, 2)
    down(1, 1)
    hidden(1, 3)
    down(1, 2)
    cross(1, 5, 6)
    down(1, 3)
    cross(1, 7)
    ret(1, 1, 0, 1)
    ret(0, 4, 2)
    cross(1, 3, 4)
    finish(0, 0, 1)
    ret(1, 2, 0, 1)
    ret(1, 1, 2)
    cross(1, 1, 2)
    finish(0, 2)
    ret(1, 3, 0, 1)
    ret(1, 2, 2)
    hand_out(0)
    cross(1, 0)
    ret(1, 4, 0, 1)
    ret(1, 3, 2)
    finish(1, 0, 1)
    ret(1, 4, 2)
    finish(1, 2)
    hand_out(1)

    for r in range(1, EXPERTS):
        phase_a(r).wait_send()
        deliver(r).wait()
        deliver_last(r).wait()
    for w in range(2):
        for i in range(9):
            x_send(w, i).wait_send()
        for g in range(4):
            gu_send(w, g).wait_send()
            hid_send(w, g).wait_send()
        for side in range(2):
            for k in range(1, 5):
                for p in range(3):
                    z_send(w, side, k, p).wait_send()
                    back_send(w, side, k, p).wait_send()
    tile = result_x[...].reshape(EXPERTS * MAIN, 128)
    rows = dot(sel[0], result[...].reshape(EXPERTS * MAIN, 2 * width))
    rows += dot(sel[1][:, :16], unfold([tile], 2 * width // 128))
    out_ref[...] = (gate_col * rows).astype(BF16)


def local(tokens, expert_ids, router_gate, w_gate, w_up, w_down):
    n_tok, dmodel = tokens.shape
    units = w_gate.shape[0]
    width = dmodel // 8
    folded = -(-3 * width // 2048) * 128
    vmem, dma = pltpu.VMEM, pltpu.SemaphoreType.DMA

    def waves(shape_of, dtype):
        return [vmem(shape_of(n), dtype) for n in ROWS]

    return pl.pallas_call(
        kernel,
        out_shape=jax.ShapeDtypeStruct((n_tok, 2 * width), BF16),
        in_specs=[pl.BlockSpec(memory_space=pltpu.VMEM)] * 3 + [pl.BlockSpec(memory_space=pl.ANY)] * 3,
        out_specs=pl.BlockSpec(memory_space=pltpu.VMEM),
        scratch_shapes=[
            vmem((2, n_tok, EXPERTS * MAIN), BF16),
            vmem((EXPERTS, MAIN, 3 * width + folded), BF16),
            vmem((EXPERTS, MAIN, 3 * width + folded), BF16),
            vmem((2, 2, 4, units, width), BF16),
            vmem((2, 4, units, width), BF16),
            vmem((EXPERTS, MAIN, 2 * width), BF16),
            vmem((EXPERTS, MAIN, 128), BF16),
            vmem((EXPERTS, MAIN, 2 * width), BF16),
            vmem((EXPERTS, MAIN, 128), BF16),
            *waves(lambda n: (RING, 4, n, width), BF16),
            *waves(lambda n: (2, RING * n, units), F32),
            *waves(lambda n: (2, RING * n, units), F32),
            *waves(lambda n: (2, RING * n, units), F32),
            *waves(lambda n: (2, RING * n, units), BF16),
            *waves(lambda n: (RING, 4, n, width), BF16),
            *waves(lambda n: (RING, n, width), BF16),
            *waves(lambda n: (2, 4, 3, n, width), BF16),
            *waves(lambda n: (3, n, width), BF16),
            *waves(lambda n: (n, width), BF16),
            dma((3, 4)), dma((3, 4)), dma((3, 4)),
            dma((8,)), dma((8,)),
            dma((2, 2, 4, 3)), dma((2, 2, 4, 3)),
            dma((2, 9)), dma((2, 9)),
            dma((2, 4)), dma((2, 4)),
            dma((2, 4)), dma((2, 4)),
            dma((2, 8)), dma((2, 8)),
            dma((2, 2, 4, 3)), dma((2, 2, 4, 3)),
            dma((2,)), dma((2,)),
            dma((8,)), dma((8,)),
            dma((8,)), dma((8,)),
        ],
        compiler_params=pltpu.CompilerParams(
            collective_id=0, has_side_effects=True, vmem_limit_bytes=60 * 2**20
        ),
        cost_estimate=pl.CostEstimate(flops=7 * 10**9, bytes_accessed=10**7, transcendentals=200000),
        name="routed_experts",
    )(tokens, expert_ids.reshape(1, n_tok), router_gate.reshape(1, n_tok), w_gate, w_up, w_down)


def solution(mesh):
    placed = (
        P("fsdp", None),
        P("fsdp", None),
        P("fsdp"),
        P(("fsdp", "ctx"), None),
        P(("fsdp", "ctx"), None),
        P(("fsdp", "ctx"), None),
    )
    return jax.shard_map(
        local, mesh=mesh, in_specs=placed, out_specs=P("fsdp", "ctx"), check_vma=False
    )
```

time: 979 us -> 140 us (0.14)
  blocking collectives: 843 us -> 0 us
  Pallas kernels: 0 us -> 137 us
  waiting for transfers between devices: 46.8 us -> 0 us
  matrix products: 33.4 us -> 0 us
  local copies, waits for them, and re-layouts: 29 us -> 1.77 us
  between operations: 13.5 us -> 0.01 us
  other arithmetic: 11.1 us -> 0 us
    all_to_all x2 -> x0, blocking collectives: 843 us -> none  [the longest x1 425 us: local(): lax.all_to_all(copies, 'fsdp', split_axis=1, concat_axis=1, tiled=True)]
    pallas_call x0 -> x1, Pallas kernels: none -> 137 us  [local(): pl.pallas_call(kernel, out_shape=jax.ShapeDtypeStruct((n_tok, 2 * width),...]
    reduce_scatter x1 -> x0, waiting for transfers between devices: 46.8 us -> none  [local(): shares = lax.psum_scatter(summed, 'ctx', scatter_dimension=2, tiled=True)]
    dot_general x3 -> x0, matrix products: 33.4 us -> none  [the longest x1 23.6 us: expert_rows(): jnp.dot(hidden, w_down, preferred_element_type=jnp.float32)]
    reshape x2 -> x0, local copies, waits for them, and re-layouts: 13.1 us -> none  [the longest x1 12.1 us: expert_rows(): return partial_value.reshape(block_shape)]
  transfers between devices with their start and end apart: 1 -> 0, of which waited for: 1 -> 0; matrix products, arithmetic and copies ran while one was open for 0% -> 0% of each run, Pallas kernels for 0% -> 0%
where the time goes in v2:
time: 140 us; the launch traced here: 139 us
  Pallas kernels  137 us (98%)
  local copies, waits for them, and re-layouts  1.77 us (1%)
    pallas_call x1, Pallas kernels, local(): pl.pallas_call(kernel, out_shape=jax.ShapeDtypeStruct((n_tok, 2 * width),...  137 us

profile of v2, /device:TPU:6, one launch (start us, length us, event | category | flops | bytes accessed | tf_op | source)
XLA Modules:
  0.0 138.9 jit_solution(2185401211683568966)
XLA Ops:
  0.0 137.2 %routed_experts.1 = bf16[128,1536]{1,0:T(8,128)(2,1)} custom-call(bf16[128,6144]{1,0:T(8,128)(2,1)} %tok_ref.1, s32[1,128]{1,0:T(1,128)} %bitcast.2, f32[1,128]{1,0:T(1,128)} %bitcast.3, bf16[168,6144]{1,0:T(8,128)(2,1)} %wg_ref.1, bf16[168,6144]{1,0:T(8,128)(2,1)} %wu_ref.1, bf16[168,6144]{1,0:T(8,128)(2,1)} %wd_ref.1), custom_call_target="tpu_custom_call" | custom-call | flops 7000000000 | bytes 10000000 | tf_op jit(solution)/shard_map/routed_experts/pallas_call | solution.py:437
  137.2 1.8 %copy.8 = bf16[128,1536]{1,0:T(8,128)(2,1)} copy(bf16[128,1536]{1,0:T(8,128)(2,1)} %routed_experts.1) | data formatting | bytes 786432

commit v3 on v2

v3 whole, which is shorter than its diff:
```python
import functools

import jax
import jax.numpy as jnp
from jax import lax
from jax.experimental import pallas as pl
from jax.experimental.pallas import tpu as pltpu
from jax.sharding import PartitionSpec as P

MESH = pl.DeviceIdType.MESH
EXPERTS = 8
MAIN = 16
RING = 8
N = 4 * MAIN
BF16, F32 = jnp.bfloat16, jnp.float32
SOURCES = ((0, 0), (0, 2), (1, 0), (1, 2), (0, 1), (0, 3), (1, 1), (1, 3))
HALF = ((0, 32), (32, 32))
ORDER = (0, -1, 1, -2, 2, -3, 3, 4)
GROUPS = (((0, 5), (5, 8)), ((0, 5), (5, 7), (7, 8)))
B_BLOCKS = 6


def nt_dot(a, b):
    return lax.dot_general(a, b, (((1,), (1,)), ((), ())), preferred_element_type=F32)


def dot(a, b):
    return jnp.dot(a, b, preferred_element_type=F32)


def transposition(shape):
    r = lax.broadcasted_iota(jnp.int32, shape, 0)
    q = lax.broadcasted_iota(jnp.int32, shape, 1)
    return (((r >> 4) == (q & 15)) & ((r & 15) == (q >> 4))).astype(F32).astype(BF16)


def fold(rows):
    tiles = []
    for lo in range(0, rows.shape[1], 2048):
        part = rows[:, lo:lo + 2048]
        n = part.shape[1] // 128
        stack = jnp.concatenate([part[:, j * 128:(j + 1) * 128] for j in range(n)], axis=0)
        tiles.append(dot(transposition((128, n * 16)), stack).astype(BF16))
    return tiles


def unfold(tiles, n_blocks):
    blocks = []
    for t, tile in enumerate(tiles):
        n = min(16, n_blocks - 16 * t)
        stack = dot(transposition((n * 16, 128)), tile).astype(BF16)
        blocks += [stack[j * 16:(j + 1) * 16] for j in range(n)]
    return jnp.concatenate(blocks, axis=1)


def widths_of(dmodel):
    wb = B_BLOCKS * 128
    wa = dmodel // 4 - wb
    return wa, wb, -(-B_BLOCKS // 2) * 128


def group_rows(w, g):
    at = 0
    for h, (lo, hi) in enumerate(GROUPS[w]):
        main, extra = (hi - lo) * N, w * (-(-(hi - lo) // 2) * 16)
        if h == g:
            return at, main + extra, extra
        at += main + extra
    return at, 0, 0


def pair_up(left, right):
    if right.shape[1] < left.shape[1]:
        pad = jnp.zeros((8, left.shape[1] - right.shape[1]), F32)
        right = jnp.concatenate([right, pad], axis=1)
    return jnp.concatenate([left, right], axis=0)


def kernel(
    tok_ref, ids_ref, gate_ref, wg_ref, wu_ref, wd_ref,
    out_ref,
    tok, sel, send, send_x, staged, staged_x, wgu_a, wgu_b, wdn_a, wdn_b,
    parcel_a, parcel_b, parcel_x, result_a, result_b, result_x, xo, yo, yxo, back_o, final_o, fxo, *rest,
):
    per_wave, sems = rest[:28], rest[28:]
    (
        x_a, x_b, gu_own, gu_out, gu_in, hid, y_a, y_b, yx, back_a, back_b, final_a, final_b, fx,
    ) = [per_wave[2 * i:2 * i + 2] for i in range(14)]
    (
        t_sem, w_sem, ws_sem, wr_sem, as_sem, ar_sem, zs_sem, zr_sem, xs_sem, xr_sem,
        gs_sem, gr_sem, hs_sem, hr_sem, ys_sem, yr_sem, bs_sem, br_sem, fs_sem, fr_sem,
        ds_sem, dr_sem,
    ) = sems
    c, f = lax.axis_index("ctx"), lax.axis_index("fsdp")
    xl, co = c // 2, c % 2
    col, z = f // RING, f % RING
    wa, wb = x_a[0].shape[3], x_b[0].shape[3]
    wo = yxo.shape[2]
    share = 2 * wa + wb

    def on_z(d):
        return (c, col * RING + (z + d + RING) % RING)

    def column(r, sign):
        dx, dy = SOURCES[r]
        return (col // 4 + dx) % 2 * 4 + (col % 4 + sign * dy + 4) % 4

    def in_column(e):
        return (c, e * RING + z)

    sibling = (c + 1 - 2 * co, f)
    across = ((c + 2) % 4, f)

    def remote(src, dst, ssem, rsem, dev):
        return pltpu.make_async_remote_copy(
            src_ref=src, dst_ref=dst, send_sem=ssem, recv_sem=rsem, device_id=dev, device_id_type=MESH
        )

    def column_of(core, blk):
        quarter = (blk % 2) * 2 + core
        return pl.multiple_of(quarter * (wa + wb) + (wa if blk >= 2 else 0), 128)

    def columns(ref, core, blk):
        return ref.at[:, pl.ds(column_of(core, blk), wb if blk >= 2 else wa)]

    own_b = pl.multiple_of((xl * 2 + co) * (wa + wb) + wa, 128)
    share_refs = [columns(tok_ref, co, 0), columns(tok_ref, co, 1), tok_ref.at[:, pl.ds(own_b, wb)]]
    spans = ((0, wa), (wa, 2 * wa), (2 * wa, share))
    get_tok = [
        pltpu.make_async_copy(share_refs[p], tok.at[:, spans[p][0]:spans[p][1]], t_sem.at[p]) for p in range(3)
    ]
    for cp in get_tok:
        cp.start()

    barrier = pltpu.get_barrier_semaphore()
    partners = [on_z(1), on_z(-1), sibling, across] + [in_column((col + i) % EXPERTS) for i in range(1, EXPERTS)]
    for dev in partners:
        pl.semaphore_signal(barrier, inc=1, device_id=dev, device_id_type=MESH)

    def weight_slot(m, unit_core, blk):
        if m == 2:
            return (wdn_b if blk >= 2 else wdn_a).at[unit_core, blk % 2]
        return (wgu_b if blk >= 2 else wgu_a).at[m, unit_core, blk % 2]

    w_refs = (wg_ref, wu_ref, wd_ref)
    own_w = [
        pltpu.make_async_copy(columns(w_refs[m], co, blk), weight_slot(m, co, blk), w_sem.at[m, blk])
        for m in range(3) for blk in range(4)
    ]
    other_w = [
        remote(
            columns(w_refs[m], 1 - co, blk), weight_slot(m, co, blk),
            ws_sem.at[m, blk], wr_sem.at[m, blk], sibling,
        )
        for m in range(3) for blk in range(4)
    ]

    n_tok = tok.shape[0]
    rows_i = lax.broadcasted_iota(jnp.int32, (n_tok, n_tok), 0)
    cols_i = lax.broadcasted_iota(jnp.int32, (n_tok, n_tok), 1)
    ids_row = ids_ref[...]
    ids_col = jnp.sum(jnp.where(rows_i == cols_i, ids_row, 0), axis=1, keepdims=True)
    same = (ids_row == ids_col) & (cols_i < rows_i)
    rank = jnp.sum(same.astype(jnp.int32), axis=1, keepdims=True)
    main = ((cols_i == ids_col * MAIN + rank) & (rank < MAIN)).astype(F32)
    last = ((cols_i == ids_col) & (rank == MAIN)).astype(F32)
    sel[0] = main.astype(BF16)
    sel[1] = last.astype(BF16)
    pack = jnp.transpose(main).astype(BF16)
    for p in range(3):
        lo, hi = spans[p]
        get_tok[p].wait()
        send[:, :, lo:hi] = dot(pack, tok[:, lo:hi]).astype(BF16).reshape(EXPERTS, MAIN, hi - lo)

    pl.semaphore_wait(barrier, len(partners))

    def phase_a(r):
        e = column(r, -1)
        return remote(send.at[e], staged.at[r], as_sem.at[0, r], ar_sem.at[0, r], in_column(e))

    def phase_a_last(r):
        e = column(r, -1)
        return remote(send_x.at[e], staged_x.at[r], as_sem.at[1, r], ar_sem.at[1, r], in_column(e))

    def x_block(w, pi, p):
        return x_b[w].at[pi, xl] if p == 2 else x_a[w].at[pi, p]

    def y_block(w, pi, p):
        if p == 3:
            return yo.at[pi, xl]
        return y_b[w].at[pi, xl] if p == 2 else y_a[w].at[pi, p]

    def land(w):
        for q in range(4):
            r = 4 * w + q
            if r:
                phase_a(r).wait_recv()
            here = send.at[col] if r == 0 else staged.at[r]
            for p in range(3):
                x_block(w, z, p)[q * MAIN:(q + 1) * MAIN, :] = here[:, spans[p][0]:spans[p][1]]

    def land_last():
        for r in range(1, EXPERTS):
            phase_a_last(r).wait_recv()
        staged_x[0] = send_x[col]
        tiles = [
            staged_x[:, :, lo:lo + 128].reshape(EXPERTS * MAIN, 128) for lo in range(0, staged_x.shape[2], 128)
        ]
        extra = unfold(tiles, share // 128).astype(F32)[:8]
        xo[z, xl, :, :wa] = pair_up(extra[:, :wa], extra[:, wa:2 * wa]).astype(BF16)
        xo[z, xl, :, wa:] = pair_up(extra[:, 2 * wa:2 * wa + wo], extra[:, 2 * wa + wo:]).astype(BF16)

    def plane(d):
        return (z + d + RING) % RING

    def z_send(w, side, k, p):
        d = 1 - 2 * side
        pi = plane(-d * (k - 1))
        blk = xo.at[pi, xl] if p == 3 else x_block(w, pi, p)
        if k == 4 and p < 3:
            blk = blk.at[pl.ds(*HALF[side])]
        return remote(blk, blk, zs_sem.at[w, side, k - 1, p], zr_sem.at[w, side, k - 1, p], on_z(d))

    def goes(w, side, k, p):
        return p < 3 or (w == 1 and not (k == 4 and side == 1))

    def x_send(w, i):
        if i < 7:
            blk = x_b[w].at[plane(ORDER[i]), xl]
        else:
            blk = x_b[w].at[plane(4), xl].at[pl.ds(*HALF[i - 7])]
        return remote(blk, blk, xs_sem.at[w, i], xr_sem.at[w, i], across)

    def x_send_last(i):
        blk = xo.at[plane(ORDER[i]), xl, :, wa:]
        return remote(blk, blk, xs_sem.at[2, i], xr_sem.at[2, i], across)

    def z_step(w, k):
        for p in (2, 3, 0, 1):
            for side in range(2):
                if k > 1 and goes(w, side, k - 1, p):
                    z_send(w, side, k - 1, p).wait_recv()
                if k < 5 and goes(w, side, k, p):
                    z_send(w, side, k, p).start()
                if p == 2 and (k > 1 or side == 0):
                    x_send(w, 2 * (k - 1) - 1 + side if k > 1 else 0).start()
                if p == 3 and w == 1 and not (k in (1, 5) and side == 1):
                    x_send_last(2 * (k - 1) - 1 + side if k > 1 else 0).start()

    def gu_send(w, g):
        lo, n, _ = group_rows(w, g)
        rows = pl.ds(lo, n)
        return remote(gu_out[w].at[:, rows], gu_in[w].at[:, rows], gs_sem.at[w, g], gr_sem.at[w, g], sibling)

    def hid_send(w, g):
        lo, n, _ = group_rows(w, g)
        mine = hid[w].at[co, pl.ds(lo, n)]
        return remote(mine, mine, hs_sem.at[w, g], hr_sem.at[w, g], sibling)

    def last_rows(pi, blk):
        if blk < 2:
            return xo[pi, xl, :, :wa].astype(F32)[8 * blk:8 * blk + 8]
        both = xo[pi, blk - 2, :, wa:].astype(F32)
        return jnp.concatenate([both[:8], both[8:, :wb - wo]], axis=1)

    def gate_up(w, g):
        lo, n, extra = group_rows(w, g)
        ids = range(*GROUPS[w][g])
        for i in ids:
            x_send(w, i).wait_recv()
            if i == 7:
                x_send(w, 8).wait_recv()
            if w == 1:
                x_send_last(i).wait_recv()
        for blk in range(4):
            xs, wgu = (x_b[w], wgu_b) if blk >= 2 else (x_a[w], wgu_a)
            parts = [xs[plane(ORDER[i]), blk % 2] for i in ids]
            if extra:
                lasts = [last_rows(plane(ORDER[i]), blk) for i in ids]
                if len(lasts) % 2:
                    lasts.append(jnp.zeros_like(lasts[0]))
                parts.append(jnp.concatenate(lasts, axis=0).astype(BF16))
            rows = jnp.concatenate(parts, axis=0)
            for m in range(2):
                for acc, u in ((gu_own[w], co), (gu_out[w], 1 - co)):
                    term = nt_dot(rows, wgu[m, u, blk % 2])
                    acc[m, lo:lo + n] = acc[m, lo:lo + n] + term if blk else term
        gu_send(w, g).start()

    def hidden(w, g):
        lo, n, _ = group_rows(w, g)
        gu_send(w, g).wait_recv()
        gate = gu_own[w][0, lo:lo + n] + gu_in[w][0, lo:lo + n]
        up = gu_own[w][1, lo:lo + n] + gu_in[w][1, lo:lo + n]
        hid[w][co, lo:lo + n] = (gate / (1.0 + jnp.exp(-gate)) * up).astype(BF16)
        hid_send(w, g).start()

    def down(w, g):
        lo, n, extra = group_rows(w, g)
        ids = range(*GROUPS[w][g])
        hid_send(w, g).wait_recv()
        lasts = {}
        for blk in (2, 3, 0, 1):
            wdn, ys = (wdn_b, y_b[w]) if blk >= 2 else (wdn_a, y_a[w])
            part = dot(hid[w][0, lo:lo + n], wdn[0, blk % 2]) + dot(hid[w][1, lo:lo + n], wdn[1, blk % 2])
            for at, i in enumerate(ids):
                ys[plane(ORDER[i]), blk % 2] = part[at * N:(at + 1) * N].astype(BF16)
                if extra:
                    at8 = len(ids) * N + 8 * at
                    mine = part[at8:at8 + 8]
                    if blk >= 2:
                        yo[plane(ORDER[i]), blk - 2, :, wa:] = pair_up(mine[:, :wo], mine[:, wo:]).astype(BF16)
                    elif blk == 0:
                        lasts[i] = mine
                    else:
                        yo[plane(ORDER[i]), xl, :, :wa] = pair_up(lasts[i], mine).astype(BF16)

    def y_send(w, i):
        return remote(y_b[w].at[plane(ORDER[i]), 1 - xl], yx[w].at[i], ys_sem.at[w, i], yr_sem.at[w, i], across)

    def y_send_last(i):
        return remote(
            yo.at[plane(ORDER[i]), 1 - xl, :, wa:], yxo.at[i], ys_sem.at[2, i], yr_sem.at[2, i], across
        )

    def cross(w, *idx):
        for i in idx:
            y_send(w, i).start()
            if w == 1:
                y_send_last(i).start()

    def add_across(w, i):
        pi = plane(ORDER[i])
        y_send(w, i).wait()
        y_b[w][pi, xl] = (y_b[w][pi, xl].astype(F32) + yx[w][i].astype(F32)).astype(BF16)

    def add_across_last(i):
        pi = plane(ORDER[i])
        y_send_last(i).wait()
        yo[pi, xl, :, wa:] = (yo[pi, xl, :, wa:].astype(F32) + yxo[i].astype(F32)).astype(BF16)

    def back_block(w, side, j, p):
        if p == 3:
            return back_o.at[side, j - 1]
        return back_b[w].at[side, j - 1] if p == 2 else back_a[w].at[side, j - 1, p]

    def back_send(w, side, j, p):
        d = 1 - 2 * side
        src = y_block(w, plane(d * (5 - j)), p)
        dst = back_block(w, side, j, p)
        if j == 1 and p < 3:
            src, dst = src.at[pl.ds(*HALF[side])], dst.at[pl.ds(*HALF[side])]
        return remote(src, dst, bs_sem.at[w, side, j - 1, p], br_sem.at[w, side, j - 1, p], on_z(d))

    def comes(w, side, j, p):
        return p < 3 or (w == 1 and not (j == 1 and side == 1))

    def ret(w, j, *ps):
        for p in ps:
            for side in range(2):
                if not comes(w, side, j, p):
                    continue
                d = 1 - 2 * side
                if p >= 2 and (j > 1 or side == 0):
                    (add_across_last if p == 3 else functools.partial(add_across, w))(ORDER.index(d * (5 - j)))
                if j > 1 and comes(w, side, j - 1, p):
                    back_send(w, side, j - 1, p).wait_recv()
                    here, came = y_block(w, plane(d * (5 - j)), p), back_block(w, side, j - 1, p)
                    if j == 2 and p < 3:
                        here, came = here.at[pl.ds(*HALF[side])], came.at[pl.ds(*HALF[side])]
                    here[...] = (here[...].astype(F32) + came[...].astype(F32)).astype(BF16)
                back_send(w, side, j, p).start()

    def f_send(w):
        return remote(final_a[w].at[1 - xl], fx[w], fs_sem.at[w], fr_sem.at[w], across)

    def f_send_last():
        return remote(final_o.at[:, :wa], fxo, fs_sem.at[2], fr_sem.at[2], across)

    def finish(w, *ps):
        for p in ps:
            if p == 2:
                add_across(w, 0)
            if p == 3:
                add_across_last(0)
            total = y_block(w, z, p)[...].astype(F32)
            for side in range(2):
                back_send(w, side, 4, p).wait_recv()
                total += back_block(w, side, 4, p)[...].astype(F32)
            if p == 3:
                final_o[...] = total.astype(BF16)
                f_send_last().start()
            elif p == 2:
                final_b[w][...] = total.astype(BF16)
            else:
                final_a[w][p] = total.astype(BF16)
                if p == 1:
                    f_send(w).start()

    def deliver(r, kind):
        parcel, result = ((parcel_a, result_a), (parcel_b, result_b), (parcel_x, result_x))[kind]
        return remote(
            parcel.at[r], result.at[col], ds_sem.at[kind, r], dr_sem.at[kind, r], in_column(column(r, 1))
        )

    def hand_out(w, kind):
        if kind == 0:
            f_send(w).wait()
            mine = (final_a[w][xl].astype(F32) + fx[w][...].astype(F32)).astype(BF16)
        else:
            mine = final_b[w][...]
        parcel, result = ((parcel_a, result_a), (parcel_b, result_b))[kind]
        parcel[4 * w:4 * w + 4] = mine.reshape(4, MAIN, mine.shape[1])
        for q in range(4):
            if w or q:
                deliver(4 * w + q, kind).start()
        if w == 0:
            result[col] = parcel[0]

    def hand_out_last():
        f_send_last().wait()
        both = final_o[:, :wa].astype(F32) + fxo[...].astype(F32)
        mine = jnp.where(xl == 0, both[:8], both[8:])
        over = final_o[:, wa:].astype(F32)
        mine = jnp.concatenate([mine, over[:8], over[8:, :wb - wo]], axis=1)
        mine = jnp.concatenate([mine, jnp.zeros_like(mine)], axis=0).astype(BF16)
        parcel_x[...] = fold(mine)[0].reshape(EXPERTS, MAIN, 128)
        for r in range(1, EXPERTS):
            deliver(r, 2).start()
        result_x[col] = parcel_x[0]

    for r in range(1, 4):
        phase_a(r).start()
    for cp in own_w + other_w:
        cp.start()
    for r in range(4, EXPERTS):
        phase_a(r).start()
    pack_last = jnp.transpose(last)[:16].astype(BF16)
    for t, tile in enumerate(fold(dot(pack_last, tok[...]).astype(BF16))):
        send_x[:, :, t * 128:(t + 1) * 128] = tile.reshape(EXPERTS, MAIN, 128)
    for r in range(1, EXPERTS):
        phase_a_last(r).start()

    land(0)
    z_step(0, 1)
    land(1)
    land_last()
    for cp in own_w + other_w:
        cp.wait()
    z_step(0, 2)
    z_step(0, 3)
    gate_up(0, 0)
    z_step(0, 4)
    z_step(1, 1)
    hidden(0, 0)
    down(0, 0)
    z_step(0, 5)
    z_step(1, 2)
    gate_up(0, 1)
    hidden(0, 1)
    z_step(1, 3)
    down(0, 1)
    cross(0, 7, 5, 6)
    gate_up(1, 0)
    z_step(1, 4)
    hidden(1, 0)
    ret(0, 1, 0, 1)
    cross(0, 3, 4)
    z_step(1, 5)
    ret(0, 1, 2)
    ret(0, 2, 0, 1)
    gate_up(1, 1)
    ret(0, 2, 2)
    ret(0, 3, 0, 1)
    gate_up(1, 2)
    hidden(1, 1)
    cross(0, 1, 2)
    hidden(1, 2)
    down(1, 0)
    ret(0, 3, 2)
    ret(0, 4, 0, 1)
    down(1, 2)
    cross(1, 7)
    ret(1, 1, 0, 1)
    cross(0, 0)
    down(1, 1)
    cross(1, 5, 6)
    ret(0, 4, 2)
    ret(1, 2, 0, 1)
    ret(1, 1, 3, 2)
    finish(0, 0, 1)
    cross(1, 3, 4)
    ret(1, 3, 0, 1)
    ret(1, 2, 3, 2)
    finish(0, 2)
    cross(1, 1, 2, 0)
    hand_out(0, 0)
    hand_out(0, 1)
    ret(1, 4, 0, 1)
    ret(1, 3, 3, 2)
    finish(1, 0, 1)
    ret(1, 4, 3, 2)
    hand_out(1, 0)
    finish(1, 3)
    finish(1, 2)
    hand_out(1, 1)
    hand_out_last()
    for r in range(1, EXPERTS):
        phase_a(r).wait_send()
        phase_a_last(r).wait_send()
    for w in range(2):
        for i in range(9):
            x_send(w, i).wait_send()
        for g in range(len(GROUPS[w])):
            gu_send(w, g).wait_send()
            hid_send(w, g).wait_send()
        for side in range(2):
            for k in range(1, 5):
                for p in range(4):
                    if goes(w, side, k, p):
                        z_send(w, side, k, p).wait_send()
                    if comes(w, side, k, p):
                        back_send(w, side, k, p).wait_send()
    for i in range(8):
        x_send_last(i).wait_send()
    for r in range(1, EXPERTS):
        deliver(r, 2).wait()
    gate_col = jnp.sum(jnp.where(rows_i == cols_i, gate_ref[...], 0.0), axis=1, keepdims=True)
    extra = unfold([result_x[...].reshape(EXPERTS * MAIN, 128)], (wa + wb) // 128)
    for kind, result, lo, hi in ((0, result_a, 0, wa), (1, result_b, wa, wa + wb)):
        for r in range(1, EXPERTS):
            deliver(r, kind).wait()
        rows = dot(sel[0], result[...].reshape(EXPERTS * MAIN, hi - lo)) + dot(sel[1][:, :16], extra[:, lo:hi])
        out_ref[:, lo:hi] = (gate_col * rows).astype(BF16)


def local(tokens, expert_ids, router_gate, w_gate, w_up, w_down):
    n_tok, dmodel = tokens.shape
    units = w_gate.shape[0]
    wa, wb, wo = widths_of(dmodel)
    share = 2 * wa + wb
    folded = -(-share // 2048) * 128
    vmem, dma = pltpu.VMEM, pltpu.SemaphoreType.DMA
    n_rows = [group_rows(w, len(GROUPS[w]))[0] for w in range(2)]

    def waves(*shape, dtype=BF16):
        return [vmem(shape, dtype)] * 2

    def per_row(*shape, dtype=F32):
        return [vmem((2, n, units), dtype) for n in n_rows]

    return pl.pallas_call(
        kernel,
        out_shape=jax.ShapeDtypeStruct((n_tok, wa + wb), BF16),
        in_specs=[pl.BlockSpec(memory_space=pl.ANY)] + [pl.BlockSpec(memory_space=pltpu.VMEM)] * 2
        + [pl.BlockSpec(memory_space=pl.ANY)] * 3,
        out_specs=pl.BlockSpec(memory_space=pltpu.VMEM),
        scratch_shapes=[
            vmem((n_tok, share), BF16),
            vmem((2, n_tok, EXPERTS * MAIN), BF16),
            vmem((EXPERTS, MAIN, share), BF16),
            vmem((EXPERTS, MAIN, folded), BF16),
            vmem((EXPERTS, MAIN, share), BF16),
            vmem((EXPERTS, MAIN, folded), BF16),
            vmem((2, 2, 2, units, wa), BF16),
            vmem((2, 2, 2, units, wb), BF16),
            vmem((2, 2, units, wa), BF16),
            vmem((2, 2, units, wb), BF16),
            vmem((EXPERTS, MAIN, wa), BF16),
            vmem((EXPERTS, MAIN, wb), BF16),
            vmem((EXPERTS, MAIN, 128), BF16),
            vmem((EXPERTS, MAIN, wa), BF16),
            vmem((EXPERTS, MAIN, wb), BF16),
            vmem((EXPERTS, MAIN, 128), BF16),
            vmem((RING, 2, 16, wa + wo), BF16),
            vmem((RING, 2, 16, wa + wo), BF16),
            vmem((RING, 16, wo), BF16),
            vmem((2, 4, 16, wa + wo), BF16),
            vmem((16, wa + wo), BF16),
            vmem((16, wa), BF16),
            *waves(RING, 2, N, wa),
            *waves(RING, 2, N, wb),
            *per_row(),
            *per_row(),
            *per_row(),
            *per_row(dtype=BF16),
            *waves(RING, 2, N, wa),
            *waves(RING, 2, N, wb),
            *waves(RING, N, wb),
            *waves(2, 4, 2, N, wa),
            *waves(2, 4, N, wb),
            *waves(2, N, wa),
            *waves(N, wb),
            *waves(N, wa),
            dma((3,)),
            dma((3, 4)), dma((3, 4)), dma((3, 4)),
            dma((2, 8)), dma((2, 8)),
            dma((2, 2, 4, 4)), dma((2, 2, 4, 4)),
            dma((3, 9)), dma((3, 9)),
            dma((2, 4)), dma((2, 4)),
            dma((2, 4)), dma((2, 4)),
            dma((3, 8)), dma((3, 8)),
            dma((2, 2, 4, 4)), dma((2, 2, 4, 4)),
            dma((3,)), dma((3,)),
            dma((3, 8)), dma((3, 8)),
        ],
        compiler_params=pltpu.CompilerParams(
            collective_id=0, has_side_effects=True, vmem_limit_bytes=60 * 2**20
        ),
        cost_estimate=pl.CostEstimate(flops=7 * 10**9, bytes_accessed=10**7, transcendentals=200000),
        name="routed_experts",
    )(tokens, expert_ids.reshape(1, n_tok), router_gate.reshape(1, n_tok), w_gate, w_up, w_down)


def solution(mesh):
    placed = (
        P("fsdp", None),
        P("fsdp", None),
        P("fsdp"),
        P(("fsdp", "ctx"), None),
        P(("fsdp", "ctx"), None),
        P(("fsdp", "ctx"), None),
    )
    return jax.shard_map(
        local, mesh=mesh, in_specs=placed, out_specs=P("fsdp", "ctx"), check_vma=False
    )
```

time: 140 us -> 131 us (0.936)
  Pallas kernels: 137 us -> 129 us
    pallas_call x1, Pallas kernels: 137 us -> 129 us  [local(): pl.pallas_call(kernel, out_shape=jax.ShapeDtypeStruct((n_tok, wa + wb), B...]
where the time goes in v3:
time: 131 us
  Pallas kernels  129 us (98%)
  local copies, waits for them, and re-layouts  1.77 us (1%)
    pallas_call x1, Pallas kernels, local(): pl.pallas_call(kernel, out_shape=jax.ShapeDtypeStruct((n_tok, wa + wb), B...  129 us

profile of v3, /device:TPU:6, one launch (start us, length us, event | category | flops | bytes accessed | tf_op | source)
XLA Modules:
  0.0 131.2 jit_solution(9007332264201218216)
XLA Ops:
  0.0 129.4 %routed_experts.1 = bf16[128,1536]{1,0:T(8,128)(2,1)} custom-call(bf16[128,6144]{1,0:T(8,128)(2,1)} %tok_ref.1, s32[1,128]{1,0:T(1,128)} %bitcast.2, f32[1,128]{1,0:T(1,128)} %bitcast.3, bf16[168,6144]{1,0:T(8,128)(2,1)} %wg_ref.1, bf16[168,6144]{1,0:T(8,128)(2,1)} %wu_ref.1, bf16[168,6144]{1,0:T(8,128)(2,1)} %wd_ref.1), custom_call_target="tpu_custom_call" | custom-call | flops 7000000000 | bytes 10000000 | tf_op jit(solution)/shard_map/routed_experts/pallas_call | solution.py:552
  129.4 1.8 %copy.8 = bf16[128,1536]{1,0:T(8,128)(2,1)} copy(bf16[128,1536]{1,0:T(8,128)(2,1)} %routed_experts.1) | data formatting | bytes 786432

commit v4 on v3

--- a/solution.py
+++ b/solution.py
@@ -14,7 +14,13 @@
 N = 4 * MAIN
 BF16, F32 = jnp.bfloat16, jnp.float32
 SOURCES = ((0, 0), (0, 2), (1, 0), (1, 2), (0, 1), (0, 3), (1, 1), (1, 3))
-HALF = ((0, 32), (32, 32))
+UNITS = (
+    (0, 0, 16, (2, 4), ((0, 16), (0, 16))),
+    (0, 16, 48, (2, 0, 1), ((16, 16), (32, 32))),
+    (1, 0, 64, (2, 3, 0, 1), ((0, 32), (32, 32))),
+)
+LAST_SPLIT = ((0, 32), (32, 32))
+CROSSED = ((0,), (1, 2), (3, 4), (5, 6), (7,))
 ORDER = (0, -1, 1, -2, 2, -3, 3, 4)
 GROUPS = (((0, 5), (5, 8)), ((0, 5), (5, 7), (7, 8)))
 B_BLOCKS = 6
@@ -74,6 +80,20 @@
         pad = jnp.zeros((8, left.shape[1] - right.shape[1]), F32)
         right = jnp.concatenate([right, pad], axis=1)
     return jnp.concatenate([left, right], axis=0)
+
+
+def moves(u, side, k, p):
+    if p not in UNITS[u][3]:
+        return False
+    if k < 4:
+        return True
+    if u == 0:
+        return side == (0 if p == 2 else 1)
+    return p != 3 or side == 0
+
+
+def rows_of(u, side, k):
+    return UNITS[u][4][side] if k == 4 else UNITS[u][1:3]
 
 
 def kernel(
@@ -87,10 +107,14 @@
         x_a, x_b, gu_own, gu_out, gu_in, hid, y_a, y_b, yx, back_a, back_b, final_a, final_b, fx,
     ) = [per_wave[2 * i:2 * i + 2] for i in range(14)]
     (
-        t_sem, w_sem, ws_sem, wr_sem, as_sem, ar_sem, zs_sem, zr_sem, xs_sem, xr_sem,
-        gs_sem, gr_sem, hs_sem, hr_sem, ys_sem, yr_sem, bs_sem, br_sem, fs_sem, fr_sem,
+        t_sem, w_sem, ws_sem, wr_sem, as_sem, ar_sem, zs_sem, zr_sems, xs_sem, xr_sem,
+        gs_sem, gr_sem, hs_sem, hr_sem, ys_sem, yr_sem, bs_sem, br_sems, fs_sem, fr_sem,
         ds_sem, dr_sem,
     ) = sems
+
+    def wait_for(sem, ref):
+        pltpu.make_async_copy(ref, ref, sem).wait()
+
     c, f = lax.axis_index("ctx"), lax.axis_index("fsdp")
     xl, co = c // 2, c % 2
     col, z = f // RING, f % RING
@@ -144,16 +168,22 @@
 
     w_refs = (wg_ref, wu_ref, wd_ref)
     own_w = [
-        pltpu.make_async_copy(columns(w_refs[m], co, blk), weight_slot(m, co, blk), w_sem.at[m, blk])
+        pltpu.make_async_copy(columns(w_refs[m], co, blk), weight_slot(m, co, blk), w_sem.at[m // 2, blk // 2])
         for m in range(3) for blk in range(4)
     ]
     other_w = [
         remote(
             columns(w_refs[m], 1 - co, blk), weight_slot(m, co, blk),
-            ws_sem.at[m, blk], wr_sem.at[m, blk], sibling,
+            ws_sem.at[m // 2, blk // 2], wr_sem.at[m // 2, blk // 2], sibling,
         )
         for m in range(3) for blk in range(4)
     ]
+
+    def weights_wait(sem):
+        for m, arrays in ((0, (wgu_a.at[:, 0], wgu_b.at[:, 0])), (1, (wdn_a.at[0], wdn_b.at[0]))):
+            for part in range(2):
+                wait_for(sem.at[m, part], arrays[part])
+
 
     n_tok = tok.shape[0]
     rows_i = lax.broadcasted_iota(jnp.int32, (n_tok, n_tok), 0)
@@ -172,36 +202,40 @@
         get_tok[p].wait()
         send[:, :, lo:hi] = dot(pack, tok[:, lo:hi]).astype(BF16).reshape(EXPERTS, MAIN, hi - lo)
 
+    for p in range(3):
+        x_block = (x_b[0].at[z, xl] if p == 2 else x_a[0].at[z, p])
+        x_block[:MAIN, :] = send[col, :, spans[p][0]:spans[p][1]]
+
     pl.semaphore_wait(barrier, len(partners))
 
     def phase_a(r):
         e = column(r, -1)
-        return remote(send.at[e], staged.at[r], as_sem.at[0, r], ar_sem.at[0, r], in_column(e))
+        return remote(send.at[e], staged.at[r], as_sem.at[0], ar_sem.at[r // 4], in_column(e))
 
     def phase_a_last(r):
         e = column(r, -1)
-        return remote(send_x.at[e], staged_x.at[r], as_sem.at[1, r], ar_sem.at[1, r], in_column(e))
-
-    def x_block(w, pi, p):
-        return x_b[w].at[pi, xl] if p == 2 else x_a[w].at[pi, p]
-
-    def y_block(w, pi, p):
+        return remote(send_x.at[e], staged_x.at[r], as_sem.at[1], ar_sem.at[2], in_column(e))
+
+    def block(arrays, w, pi, p, rows):
+        a, b, last = arrays
         if p == 3:
-            return yo.at[pi, xl]
-        return y_b[w].at[pi, xl] if p == 2 else y_a[w].at[pi, p]
+            return last.at[pi, xl]
+        if p == 2:
+            return b[w].at[pi, xl, pl.ds(*rows)]
+        return a[w].at[pi, :, pl.ds(*rows)] if p == 4 else a[w].at[pi, p, pl.ds(*rows)]
+
+    x_all, y_all = (x_a, x_b, xo), (y_a, y_b, yo)
 
     def land(w):
-        for q in range(4):
-            r = 4 * w + q
-            if r:
-                phase_a(r).wait_recv()
-            here = send.at[col] if r == 0 else staged.at[r]
-            for p in range(3):
-                x_block(w, z, p)[q * MAIN:(q + 1) * MAIN, :] = here[:, spans[p][0]:spans[p][1]]
+        first = 1 - w
+        wait_for(ar_sem.at[w], staged.at[pl.ds(first, 4 - first)])
+        for p in range(3):
+            got = staged[4 * w + first:4 * w + 4, :, spans[p][0]:spans[p][1]]
+            here = block(x_all, w, z, p, (first * MAIN, (4 - first) * MAIN))
+            here[...] = got.reshape((4 - first) * MAIN, got.shape[2])
 
     def land_last():
-        for r in range(1, EXPERTS):
-            phase_a_last(r).wait_recv()
+        wait_for(ar_sem.at[2], staged_x.at[pl.ds(1, 7)])
         staged_x[0] = send_x[col]
         tiles = [
             staged_x[:, :, lo:lo + 128].reshape(EXPERTS * MAIN, 128) for lo in range(0, staged_x.shape[2], 128)
@@ -213,49 +247,54 @@
     def plane(d):
         return (z + d + RING) % RING
 
-    def z_send(w, side, k, p):
+    def lane(sems_of, u, side, k, p):
+        return sems_of[u].at[side, k - 1, UNITS[u][3].index(p)]
+
+    def sent(sem, w, p):
+        return sem.at[4 if p == 3 else 2 * w + int(p == 2)]
+
+    def z_send(u, side, k, p):
         d = 1 - 2 * side
-        pi = plane(-d * (k - 1))
-        blk = xo.at[pi, xl] if p == 3 else x_block(w, pi, p)
-        if k == 4 and p < 3:
-            blk = blk.at[pl.ds(*HALF[side])]
-        return remote(blk, blk, zs_sem.at[w, side, k - 1, p], zr_sem.at[w, side, k - 1, p], on_z(d))
-
-    def goes(w, side, k, p):
-        return p < 3 or (w == 1 and not (k == 4 and side == 1))
+        w = UNITS[u][0]
+        blk = block(x_all, w, plane(-d * (k - 1)), p, rows_of(u, side, k))
+        return remote(blk, blk, sent(zs_sem, w, p), lane(zr_sems, u, side, k, p), on_z(d))
+
+    def group_of(w, i):
+        return [g for g, (lo, hi) in enumerate(GROUPS[w]) if lo <= i < hi][0]
 
     def x_send(w, i):
         if i < 7:
             blk = x_b[w].at[plane(ORDER[i]), xl]
         else:
-            blk = x_b[w].at[plane(4), xl].at[pl.ds(*HALF[i - 7])]
-        return remote(blk, blk, xs_sem.at[w, i], xr_sem.at[w, i], across)
+            blk = x_b[w].at[plane(4), xl].at[pl.ds(*LAST_SPLIT[i - 7])]
+        return remote(blk, blk, xs_sem.at[w], xr_sem.at[w, group_of(w, min(i, 7))], across)
 
     def x_send_last(i):
         blk = xo.at[plane(ORDER[i]), xl, :, wa:]
-        return remote(blk, blk, xs_sem.at[2, i], xr_sem.at[2, i], across)
-
-    def z_step(w, k):
-        for p in (2, 3, 0, 1):
+        return remote(blk, blk, xs_sem.at[2], xr_sem.at[2, group_of(1, i)], across)
+
+    def z_step(u, k):
+        w = UNITS[u][0]
+        for p in UNITS[u][3]:
             for side in range(2):
-                if k > 1 and goes(w, side, k - 1, p):
-                    z_send(w, side, k - 1, p).wait_recv()
-                if k < 5 and goes(w, side, k, p):
-                    z_send(w, side, k, p).start()
-                if p == 2 and (k > 1 or side == 0):
+                if k > 1 and moves(u, side, k - 1, p):
+                    z_send(u, side, k - 1, p).wait_recv()
+                if k < 5 and moves(u, side, k, p):
+                    z_send(u, side, k, p).start()
+                if u and p == 2 and (k > 1 or side == 0):
                     x_send(w, 2 * (k - 1) - 1 + side if k > 1 else 0).start()
-                if p == 3 and w == 1 and not (k in (1, 5) and side == 1):
+                if p == 3 and not (k in (1, 5) and side == 1):
                     x_send_last(2 * (k - 1) - 1 + side if k > 1 else 0).start()
 
     def gu_send(w, g):
         lo, n, _ = group_rows(w, g)
         rows = pl.ds(lo, n)
-        return remote(gu_out[w].at[:, rows], gu_in[w].at[:, rows], gs_sem.at[w, g], gr_sem.at[w, g], sibling)
+        return remote(gu_out[w].at[:, rows], gu_in[w].at[:, rows], gs_sem.at[w], gr_sem.at[w, g], sibling)
 
     def hid_send(w, g):
         lo, n, _ = group_rows(w, g)
         mine = hid[w].at[co, pl.ds(lo, n)]
-        return remote(mine, mine, hs_sem.at[w, g], hr_sem.at[w, g], sibling)
+        return remote(mine, mine, hs_sem.at[w], hr_sem.at[w, g], sibling)
 
     def last_rows(pi, blk):
         if blk < 2:
@@ -266,12 +305,9 @@
     def gate_up(w, g):
         lo, n, extra = group_rows(w, g)
         ids = range(*GROUPS[w][g])
-        for i in ids:
-            x_send(w, i).wait_recv()
-            if i == 7:
-                x_send(w, 8).wait_recv()
-            if w == 1:
-                x_send_last(i).wait_recv()
+        wait_for(xr_sem.at[w, g], yx[w].at[pl.ds(0, len(ids))])
+        if w == 1:
+            wait_for(xr_sem.at[2, g], yxo.at[pl.ds(0, len(ids))])
         for blk in range(4):
             xs, wgu = (x_b[w], wgu_b) if blk >= 2 else (x_a[w], wgu_a)
             parts = [xs[plane(ORDER[i]), blk % 2] for i in ids]
@@ -315,12 +351,17 @@
                     else:
                         yo[plane(ORDER[i]), xl, :, :wa] = pair_up(lasts[i], mine).astype(BF16)
 
+    def far(i):
+        return [n for n, ids in enumerate(CROSSED) if i in ids][0]
+
     def y_send(w, i):
-        return remote(y_b[w].at[plane(ORDER[i]), 1 - xl], yx[w].at[i], ys_sem.at[w, i], yr_sem.at[w, i], across)
+        return remote(
+            y_b[w].at[plane(ORDER[i]), 1 - xl], yx[w].at[i], ys_sem.at[w], yr_sem.at[w, far(i)], across
+        )
 
     def y_send_last(i):
         return remote(
-            yo.at[plane(ORDER[i]), 1 - xl, :, wa:], yxo.at[i], ys_sem.at[2, i], yr_sem.at[2, i], across
+            yo.at[plane(ORDER[i]), 1 - xl, :, wa:], yxo.at[i], ys_sem.at[2], yr_sem.at[2, far(i)], across
         )
 
     def cross(w, *idx):
@@ -329,93 +370,104 @@
             if w == 1:
                 y_send_last(i).start()
 
-    def add_across(w, i):
-        pi = plane(ORDER[i])
-        y_send(w, i).wait()
-        y_b[w][pi, xl] = (y_b[w][pi, xl].astype(F32) + yx[w][i].astype(F32)).astype(BF16)
-
-    def add_across_last(i):
-        pi = plane(ORDER[i])
-        y_send_last(i).wait()
-        yo[pi, xl, :, wa:] = (yo[pi, xl, :, wa:].astype(F32) + yxo[i].astype(F32)).astype(BF16)
-
-    def back_block(w, side, j, p):
+    crossed = set()
+
+    def add_across(w, p, n):
+        if (w, p, n) in crossed:
+            return
+        crossed.add((w, p, n))
+        ids = CROSSED[n]
+        came = yxo if p == 3 else yx[w]
+        wait_for(yr_sem.at[2 if p == 3 else w, n], came.at[pl.ds(ids[0], len(ids))])
+        for i in ids:
+            pi = plane(ORDER[i])
+            here = yo.at[pi, xl, :, pl.ds(wa, wo)] if p == 3 else y_b[w].at[pi, xl]
+            here[...] = (here[...].astype(F32) + came[i].astype(F32)).astype(BF16)
+
+    def back_block(u, side, j, p):
+        w, rows = UNITS[u][0], rows_of(u, side, 5 - j)
         if p == 3:
             return back_o.at[side, j - 1]
-        return back_b[w].at[side, j - 1] if p == 2 else back_a[w].at[side, j - 1, p]
-
-    def back_send(w, side, j, p):
+        if p == 2:
+            return back_b[w].at[side, j - 1, pl.ds(*rows)]
+        if p == 4:
+            return back_a[w].at[side, j - 1, :, pl.ds(*rows)]
+        return back_a[w].at[side, j - 1, p, pl.ds(*rows)]
+
+    def back_send(u, side, j, p):
         d = 1 - 2 * side
-        src = y_block(w, plane(d * (5 - j)), p)
-        dst = back_block(w, side, j, p)
-        if j == 1 and p < 3:
-            src, dst = src.at[pl.ds(*HALF[side])], dst.at[pl.ds(*HALF[side])]
-        return remote(src, dst, bs_sem.at[w, side, j - 1, p], br_sem.at[w, side, j - 1, p], on_z(d))
-
-    def comes(w, side, j, p):
-        return p < 3 or (w == 1 and not (j == 1 and side == 1))
-
-    def ret(w, j, *ps):
+        w = UNITS[u][0]
+        here = block(y_all, w, plane(d * (5 - j)), p, rows_of(u, side, 5 - j))
+        return remote(here, back_block(u, side, j, p), sent(bs_sem, w, p), lane(br_sems, u, side, j, p), on_z(d))
+
+    def ret(u, j, *ps):
+        w = UNITS[u][0]
         for p in ps:
             for side in range(2):
-                if not comes(w, side, j, p):
+                if not moves(u, side, 5 - j, p):
                     continue
                 d = 1 - 2 * side
-                if p >= 2 and (j > 1 or side == 0):
-                    (add_across_last if p == 3 else functools.partial(add_across, w))(ORDER.index(d * (5 - j)))
-                if j > 1 and comes(w, side, j - 1, p):
-                    back_send(w, side, j - 1, p).wait_recv()
-                    here, came = y_block(w, plane(d * (5 - j)), p), back_block(w, side, j - 1, p)
-                    if j == 2 and p < 3:
-                        here, came = here.at[pl.ds(*HALF[side])], came.at[pl.ds(*HALF[side])]
-                    here[...] = (here[...].astype(F32) + came[...].astype(F32)).astype(BF16)
-                back_send(w, side, j, p).start()
-
-    def f_send(w):
-        return remote(final_a[w].at[1 - xl], fx[w], fs_sem.at[w], fr_sem.at[w], across)
+                if p in (2, 3):
+                    add_across(w, p, 5 - j)
+                if j > 1 and moves(u, side, 6 - j, p):
+                    back_send(u, side, j - 1, p).wait_recv()
+                    here = block(y_all, w, plane(d * (5 - j)), p, rows_of(u, side, 6 - j))
+                    here[...] = (here[...].astype(F32) + back_block(u, side, j - 1, p)[...].astype(F32)).astype(BF16)
+                back_send(u, side, j, p).start()
+
+    def f_send(u):
+        w, lo, n = UNITS[u][:3]
+        return remote(
+            final_a[w].at[1 - xl, pl.ds(lo, n)], fx[w].at[pl.ds(lo, n)], fs_sem.at[u], fr_sem.at[u], across
+        )
 
     def f_send_last():
-        return remote(final_o.at[:, :wa], fxo, fs_sem.at[2], fr_sem.at[2], across)
-
-    def finish(w, *ps):
+        return remote(final_o.at[:, :wa], fxo, fs_sem.at[3], fr_sem.at[3], across)
+
+    def finish(u, *ps):
+        w, lo, n = UNITS[u][:3]
         for p in ps:
-            if p == 2:
-                add_across(w, 0)
+            if p in (2, 3):
+                add_across(w, p, 0)
+            total = block(y_all, w, z, p, (lo, n))[...].astype(F32)
+            for side in range(2):
+                back_send(u, side, 4, p).wait_recv()
+                total += back_block(u, side, 4, p)[...].astype(F32)
+            total = total.astype(BF16)
             if p == 3:
-                add_across_last(0)
-            total = y_block(w, z, p)[...].astype(F32)
-            for side in range(2):
-                back_send(w, side, 4, p).wait_recv()
-                total += back_block(w, side, 4, p)[...].astype(F32)
-            if p == 3:
-                final_o[...] = total.astype(BF16)
+                final_o[...] = total
                 f_send_last().start()
             elif p == 2:
-                final_b[w][...] = total.astype(BF16)
+                final_b[w][lo:lo + n] = total
             else:
-                final_a[w][p] = total.astype(BF16)
-                if p == 1:
-                    f_send(w).start()
+                if p == 4:
+                    final_a[w][:, lo:lo + n] = total
+                else:
+                    final_a[w][p, lo:lo + n] = total
+                if p:
+                    f_send(u).start()
 
     def deliver(r, kind):
         parcel, result = ((parcel_a, result_a), (parcel_b, result_b), (parcel_x, result_x))[kind]
         return remote(
-            parcel.at[r], result.at[col], ds_sem.at[kind, r], dr_sem.at[kind, r], in_column(column(r, 1))
+            parcel.at[r], result.at[col], ds_sem.at[kind], dr_sem.at[kind], in_column(column(r, 1))
         )
 
-    def hand_out(w, kind):
+    def hand_out(u, kind):
+        w, lo, n = UNITS[u][:3]
         if kind == 0:
-            f_send(w).wait()
-            mine = (final_a[w][xl].astype(F32) + fx[w][...].astype(F32)).astype(BF16)
+            f_send(u).wait()
+            mine = (final_a[w][xl, lo:lo + n].astype(F32) + fx[w][lo:lo + n].astype(F32)).astype(BF16)
         else:
-            mine = final_b[w][...]
-        parcel, result = ((parcel_a, result_a), (parcel_b, result_b))[kind]
-        parcel[4 * w:4 * w + 4] = mine.reshape(4, MAIN, mine.shape[1])
-        for q in range(4):
-            if w or q:
-                deliver(4 * w + q, kind).start()
-        if w == 0:
-            result[col] = parcel[0]
+            mine = final_b[w][lo:lo + n]
+        if u == 0:
+            ((result_a, result_b)[kind])[col] = mine
+            return
+        parcel = (parcel_a, parcel_b)[kind]
+        first = 4 * w + lo // MAIN
+        parcel[first:first + n // MAIN] = mine.reshape(n // MAIN, MAIN, mine.shape[1])
+        for r in range(first, first + n // MAIN):
+            deliver(r, kind).start()
 
     def hand_out_last():
         f_send_last().wait()
@@ -431,107 +483,124 @@
 
     for r in range(1, 4):
         phase_a(r).start()
-    for cp in own_w + other_w:
-        cp.start()
-    for r in range(4, EXPERTS):
-        phase_a(r).start()
-    pack_last = jnp.transpose(last)[:16].astype(BF16)
-    for t, tile in enumerate(fold(dot(pack_last, tok[...]).astype(BF16))):
-        send_x[:, :, t * 128:(t + 1) * 128] = tile.reshape(EXPERTS, MAIN, 128)
-    for r in range(1, EXPERTS):
-        phase_a_last(r).start()
-
+
+    def start_rest():
+        for cp in own_w + other_w:
+            cp.start()
+        for r in range(4, EXPERTS):
+            phase_a(r).start()
+        pack_last = jnp.transpose(last)[:16].astype(BF16)
+        for t, tile in enumerate(fold(dot(pack_last, tok[...]).astype(BF16))):
+            send_x[:, :, t * 128:(t + 1) * 128] = tile.reshape(EXPERTS, MAIN, 128)
+        for r in range(1, EXPERTS):
+            phase_a_last(r).start()
+
+    z_step(0, 1)
+    start_rest()
+    z_step(0, 2)
+    z_step(0, 3)
     land(0)
-    z_step(0, 1)
+    z_step(1, 1)
+    z_step(0, 4)
+    z_step(0, 5)
     land(1)
     land_last()
-    for cp in own_w + other_w:
-        cp.wait()
-    z_step(0, 2)
-    z_step(0, 3)
+    weights_wait(w_sem)
+    weights_wait(wr_sem)
+    z_step(1, 2)
+    z_step(1, 3)
     gate_up(0, 0)
-    z_step(0, 4)
-    z_step(1, 1)
+    z_step(1, 4)
+    z_step(2, 1)
     hidden(0, 0)
     down(0, 0)
-    z_step(0, 5)
-    z_step(1, 2)
+    z_step(1, 5)
+    z_step(2, 2)
     gate_up(0, 1)
     hidden(0, 1)
-    z_step(1, 3)
+    z_step(2, 3)
     down(0, 1)
     cross(0, 7, 5, 6)
     gate_up(1, 0)
-    z_step(1, 4)
+    z_step(2, 4)
     hidden(1, 0)
-    ret(0, 1, 0, 1)
+    ret(1, 1, 0, 1)
     cross(0, 3, 4)
-    z_step(1, 5)
-    ret(0, 1, 2)
-    ret(0, 2, 0, 1)
+    z_step(2, 5)
+    ret(1, 1, 2)
+    ret(1, 2, 0, 1)
     gate_up(1, 1)
-    ret(0, 2, 2)
-    ret(0, 3, 0, 1)
+    ret(1, 2, 2)
+    ret(1, 3, 0, 1)
     gate_up(1, 2)
     hidden(1, 1)
     cross(0, 1, 2)
     hidden(1, 2)
     down(1, 0)
-    ret(0, 3, 2)
-    ret(0, 4, 0, 1)
+    ret(1, 3, 2)
+    ret(1, 4, 0, 1)
     down(1, 2)
     cross(1, 7)
-    ret(1, 1, 0, 1)
+    ret(2, 1, 0, 1)
     cross(0, 0)
     down(1, 1)
     cross(1, 5, 6)
+    ret(1, 4, 2)
+    ret(2, 2, 0, 1)
+    ret(2, 1, 3, 2)
+    finish(1, 0, 1)
+    cross(1, 3, 4)
+    ret(0, 1, 4)
+    ret(2, 3, 0, 1)
+    ret(2, 2, 3, 2)
+    ret(0, 1, 2)
+    ret(0, 2, 4)
+    finish(1, 2)
+    cross(1, 1, 2, 0)
+    hand_out(1, 0)
+    hand_out(1, 1)
+    ret(2, 4, 0, 1)
+    ret(2, 3, 3, 2)
+    ret(0, 2, 2)
+    ret(0, 3, 4)
+    finish(2, 0, 1)
+    ret(2, 4, 3, 2)
+    ret(0, 3, 2)
+    ret(0, 4, 4)
+    hand_out(2, 0)
+    finish(2, 3)
+    finish(2, 2)
+    hand_out(2, 1)
     ret(0, 4, 2)
-    ret(1, 2, 0, 1)
-    ret(1, 1, 3, 2)
-    finish(0, 0, 1)
-    cross(1, 3, 4)
-    ret(1, 3, 0, 1)
-    ret(1, 2, 3, 2)
-    finish(0, 2)
-    cross(1, 1, 2, 0)
+    hand_out_last()
+    finish(0, 4, 2)
     hand_out(0, 0)
     hand_out(0, 1)
-    ret(1, 4, 0, 1)
-    ret(1, 3, 3, 2)
-    finish(1, 0, 1)
-    ret(1, 4, 3, 2)
-    hand_out(1, 0)
-    finish(1, 3)
-    finish(1, 2)
-    hand_out(1, 1)
-    hand_out_last()
-    for r in range(1, EXPERTS):
-        phase_a(r).wait_send()
-        phase_a_last(r).wait_send()
+    seven = pl.ds(0, 7)
+    wait_for(as_sem.at[0], send.at[seven])
+    wait_for(as_sem.at[1], send_x.at[seven])
+    weights_wait(ws_sem)
     for w in range(2):
-        for i in range(9):
-            x_send(w, i).wait_send()
-        for g in range(len(GROUPS[w])):
-            gu_send(w, g).wait_send()
-            hid_send(w, g).wait_send()
-        for side in range(2):
-            for k in range(1, 5):
-                for p in range(4):
-                    if goes(w, side, k, p):
-                        z_send(w, side, k, p).wait_send()
-                    if comes(w, side, k, p):
-                        back_send(w, side, k, p).wait_send()
-    for i in range(8):
-        x_send_last(i).wait_send()
-    for r in range(1, EXPERTS):
-        deliver(r, 2).wait()
+        wait_for(xs_sem.at[w], yx[w])
+        wait_for(ys_sem.at[w], yx[w])
+        wait_for(gs_sem.at[w], gu_out[w])
+        wait_for(hs_sem.at[w], hid[w].at[0])
+        for sem in (zs_sem, bs_sem):
+            wait_for(sem.at[2 * w], x_a[w].at[seven])
+            wait_for(sem.at[2 * w + 1], yx[w].at[seven])
+    for sem in (zs_sem, bs_sem):
+        wait_for(sem.at[4], xo.at[seven, 0])
+    for sem in (xs_sem, ys_sem):
+        wait_for(sem.at[2], yxo)
     gate_col = jnp.sum(jnp.where(rows_i == cols_i, gate_ref[...], 0.0), axis=1, keepdims=True)
+    wait_for(dr_sem.at[2], result_x.at[seven])
     extra = unfold([result_x[...].reshape(EXPERTS * MAIN, 128)], (wa + wb) // 128)
     for kind, result, lo, hi in ((0, result_a, 0, wa), (1, result_b, wa, wa + wb)):
-        for r in range(1, EXPERTS):
-            deliver(r, kind).wait()
+        wait_for(dr_sem.at[kind], result.at[seven])
         rows = dot(sel[0], result[...].reshape(EXPERTS * MAIN, hi - lo)) + dot(sel[1][:, :16], extra[:, lo:hi])
         out_ref[:, lo:hi] = (gate_col * rows).astype(BF16)
+    for kind, parcel in enumerate((parcel_a, parcel_b, parcel_x)):
+        wait_for(ds_sem.at[kind], parcel.at[seven])
 
 
 def local(tokens, expert_ids, router_gate, w_gate, w_up, w_down):
@@ -593,16 +662,16 @@
             *waves(N, wb),
             *waves(N, wa),
             dma((3,)),
-            dma((3, 4)), dma((3, 4)), dma((3, 4)),
-            dma((2, 8)), dma((2, 8)),
-            dma((2, 2, 4, 4)), dma((2, 2, 4, 4)),
-            dma((3, 9)), dma((3, 9)),
-            dma((2, 4)), dma((2, 4)),
-            dma((2, 4)), dma((2, 4)),
-            dma((3, 8)), dma((3, 8)),
-            dma((2, 2, 4, 4)), dma((2, 2, 4, 4)),
+            dma((2, 2)), dma((2, 2)), dma((2, 2)),
+            dma((2,)), dma((3,)),
+            dma((5,)), [dma((2, 4, len(unit[3]))) for unit in UNITS],
+            dma((3,)), dma((3, 3)),
+            dma((2,)), dma((2, 3)),
+            dma((2,)), dma((2, 3)),
+            dma((3,)), dma((3, 5)),
+            dma((5,)), [dma((2, 4, len(unit[3]))) for unit in UNITS],
+            dma((4,)), dma((4,)),
             dma((3,)), dma((3,)),
-            dma((3, 8)), dma((3, 8)),
         ],
         compiler_params=pltpu.CompilerParams(
             collective_id=0, has_side_effects=True, vmem_limit_bytes=60 * 2**20

time: 131 us -> 129 us (0.985)
  Pallas kernels: 129 us -> 127 us
    pallas_call x1, Pallas kernels: 129 us -> 127 us  [local(): pl.pallas_call(kernel, out_shape=jax.ShapeDtypeStruct((n_tok, wa + wb), B...]
where the time goes in v4:
time: 129 us
  Pallas kernels  127 us (98%)
  local copies, waits for them, and re-layouts  1.77 us (1%)
    pallas_call x1, Pallas kernels, local(): pl.pallas_call(kernel, out_shape=jax.ShapeDtypeStruct((n_tok, wa + wb), B...  127 us

profile of v4, /device:TPU:6, one launch (start us, length us, event | category | flops | bytes accessed | tf_op | source)
XLA Modules:
  0.0 128.8 jit_solution(228175882906679259)
XLA Ops:
  0.0 127.0 %routed_experts.1 = bf16[128,1536]{1,0:T(8,128)(2,1)} custom-call(bf16[128,6144]{1,0:T(8,128)(2,1)} %tok_ref.1, s32[1,128]{1,0:T(1,128)} %bitcast.2, f32[1,128]{1,0:T(1,128)} %bitcast.3, bf16[168,6144]{1,0:T(8,128)(2,1)} %wg_ref.1, bf16[168,6144]{1,0:T(8,128)(2,1)} %wu_ref.1, bf16[168,6144]{1,0:T(8,128)(2,1)} %wd_ref.1), custom_call_target="tpu_custom_call" | custom-call | flops 7000000000 | bytes 10000000 | tf_op jit(solution)/shard_map/routed_experts/pallas_call | solution.py:621
  127.0 1.8 %copy.8 = bf16[128,1536]{1,0:T(8,128)(2,1)} copy(bf16[128,1536]{1,0:T(8,128)(2,1)} %routed_experts.1) | data formatting | bytes 786432

commit v5 on v4

--- a/solution.py
+++ b/solution.py
@@ -88,7 +88,7 @@
     if k < 4:
         return True
     if u == 0:
-        return side == (0 if p == 2 else 1)
+        return side == 0
     return p != 3 or side == 0
 
 
@@ -273,18 +273,11 @@
         blk = xo.at[plane(ORDER[i]), xl, :, wa:]
         return remote(blk, blk, xs_sem.at[2], xr_sem.at[2, group_of(1, i)], across)
 
-    def z_step(u, k):
-        w = UNITS[u][0]
-        for p in UNITS[u][3]:
-            for side in range(2):
-                if k > 1 and moves(u, side, k - 1, p):
-                    z_send(u, side, k - 1, p).wait_recv()
-                if k < 5 and moves(u, side, k, p):
-                    z_send(u, side, k, p).start()
-                if u and p == 2 and (k > 1 or side == 0):
-                    x_send(w, 2 * (k - 1) - 1 + side if k > 1 else 0).start()
-                if p == 3 and not (k in (1, 5) and side == 1):
-                    x_send_last(2 * (k - 1) - 1 + side if k > 1 else 0).start()
+    def z_task(u, side, k, p):
+        if k > 1 and moves(u, side, k - 1, p):
+            z_send(u, side, k - 1, p).wait_recv()
+        if k < 5 and moves(u, side, k, p):
+            z_send(u, side, k, p).start()
 
     def gu_send(w, g):
         lo, n, _ = group_rows(w, g)
@@ -302,26 +295,27 @@
         both = xo[pi, blk - 2, :, wa:].astype(F32)
         return jnp.concatenate([both[:8], both[8:, :wb - wo]], axis=1)
 
-    def gate_up(w, g):
+    def gate_up(w, g, blk):
         lo, n, extra = group_rows(w, g)
         ids = range(*GROUPS[w][g])
-        wait_for(xr_sem.at[w, g], yx[w].at[pl.ds(0, len(ids))])
-        if w == 1:
-            wait_for(xr_sem.at[2, g], yxo.at[pl.ds(0, len(ids))])
-        for blk in range(4):
-            xs, wgu = (x_b[w], wgu_b) if blk >= 2 else (x_a[w], wgu_a)
-            parts = [xs[plane(ORDER[i]), blk % 2] for i in ids]
-            if extra:
-                lasts = [last_rows(plane(ORDER[i]), blk) for i in ids]
-                if len(lasts) % 2:
-                    lasts.append(jnp.zeros_like(lasts[0]))
-                parts.append(jnp.concatenate(lasts, axis=0).astype(BF16))
-            rows = jnp.concatenate(parts, axis=0)
-            for m in range(2):
-                for acc, u in ((gu_own[w], co), (gu_out[w], 1 - co)):
-                    term = nt_dot(rows, wgu[m, u, blk % 2])
-                    acc[m, lo:lo + n] = acc[m, lo:lo + n] + term if blk else term
-        gu_send(w, g).start()
+        if blk == 2:
+            wait_for(xr_sem.at[w, g], yx[w].at[pl.ds(0, len(ids))])
+            if w == 1:
+                wait_for(xr_sem.at[2, g], yxo.at[pl.ds(0, len(ids))])
+        xs, wgu = (x_b[w], wgu_b) if blk >= 2 else (x_a[w], wgu_a)
+        parts = [xs[plane(ORDER[i]), blk % 2] for i in ids]
+        if extra:
+            lasts = [last_rows(plane(ORDER[i]), blk) for i in ids]
+            if len(lasts) % 2:
+                lasts.append(jnp.zeros_like(lasts[0]))
+            parts.append(jnp.concatenate(lasts, axis=0).astype(BF16))
+        rows = jnp.concatenate(parts, axis=0)
+        for m in range(2):
+            for acc, u in ((gu_own[w], co), (gu_out[w], 1 - co)):
+                term = nt_dot(rows, wgu[m, u, blk % 2])
+                acc[m, lo:lo + n] = acc[m, lo:lo + n] + term if blk else term
+        if blk == 3:
+            gu_send(w, g).start()
 
     def hidden(w, g):
         lo, n, _ = group_rows(w, g)
@@ -331,12 +325,13 @@
         hid[w][co, lo:lo + n] = (gate / (1.0 + jnp.exp(-gate)) * up).astype(BF16)
         hid_send(w, g).start()
 
-    def down(w, g):
+    def down(w, g, kind):
         lo, n, extra = group_rows(w, g)
         ids = range(*GROUPS[w][g])
-        hid_send(w, g).wait_recv()
+        if kind == "b":
+            hid_send(w, g).wait_recv()
         lasts = {}
-        for blk in (2, 3, 0, 1):
+        for blk in ((2, 3) if kind == "b" else (0, 1)):
             wdn, ys = (wdn_b, y_b[w]) if blk >= 2 else (wdn_a, y_a[w])
             part = dot(hid[w][0, lo:lo + n], wdn[0, blk % 2]) + dot(hid[w][1, lo:lo + n], wdn[1, blk % 2])
             for at, i in enumerate(ids):
@@ -400,20 +395,15 @@
         here = block(y_all, w, plane(d * (5 - j)), p, rows_of(u, side, 5 - j))
         return remote(here, back_block(u, side, j, p), sent(bs_sem, w, p), lane(br_sems, u, side, j, p), on_z(d))
 
-    def ret(u, j, *ps):
-        w = UNITS[u][0]
-        for p in ps:
-            for side in range(2):
-                if not moves(u, side, 5 - j, p):
-                    continue
-                d = 1 - 2 * side
-                if p in (2, 3):
-                    add_across(w, p, 5 - j)
-                if j > 1 and moves(u, side, 6 - j, p):
-                    back_send(u, side, j - 1, p).wait_recv()
-                    here = block(y_all, w, plane(d * (5 - j)), p, rows_of(u, side, 6 - j))
-                    here[...] = (here[...].astype(F32) + back_block(u, side, j - 1, p)[...].astype(F32)).astype(BF16)
-                back_send(u, side, j, p).start()
+    def ret_task(u, side, j, p):
+        w, d = UNITS[u][0], 1 - 2 * side
+        if p in (2, 3):
+            add_across(w, p, 5 - j)
+        if j > 1 and moves(u, side, 6 - j, p):
+            back_send(u, side, j - 1, p).wait_recv()
+            here = block(y_all, w, plane(d * (5 - j)), p, rows_of(u, side, 6 - j))
+            here[...] = (here[...].astype(F32) + back_block(u, side, j - 1, p)[...].astype(F32)).astype(BF16)
+        back_send(u, side, j, p).start()
 
     def f_send(u):
         w, lo, n = UNITS[u][:3]
@@ -495,87 +485,262 @@
         for r in range(1, EXPERTS):
             phase_a_last(r).start()
 
-    z_step(0, 1)
+    z_task(0, 0, 1, 2)
+    z_task(0, 1, 1, 2)
+    z_task(0, 1, 1, 4)
+    z_task(0, 0, 1, 4)
     start_rest()
-    z_step(0, 2)
-    z_step(0, 3)
+    z_task(0, 0, 2, 2)
+    z_task(0, 1, 2, 2)
+    z_task(0, 0, 2, 4)
+    z_task(0, 1, 2, 4)
+    z_task(0, 0, 3, 2)
+    z_task(0, 1, 3, 2)
+    z_task(0, 0, 3, 4)
+    z_task(0, 1, 3, 4)
+    z_task(0, 0, 4, 2)
+    z_task(0, 1, 4, 2)
     land(0)
-    z_step(1, 1)
-    z_step(0, 4)
-    z_step(0, 5)
+    z_task(1, 0, 1, 2)
+    z_task(1, 1, 1, 2)
+    x_send(0, 0).start()
+    z_task(1, 1, 1, 0)
+    z_task(1, 0, 1, 0)
+    z_task(1, 0, 1, 1)
+    z_task(0, 0, 4, 4)
+    z_task(1, 1, 1, 1)
+    z_task(0, 1, 4, 4)
+    z_task(0, 0, 5, 2)
     land(1)
     land_last()
     weights_wait(w_sem)
     weights_wait(wr_sem)
-    z_step(1, 2)
-    z_step(1, 3)
-    gate_up(0, 0)
-    z_step(1, 4)
-    z_step(2, 1)
+    z_task(1, 0, 2, 2)
+    x_send(0, 1).start()
+    z_task(1, 1, 2, 2)
+    x_send(0, 2).start()
+    z_task(1, 0, 2, 0)
+    z_task(1, 1, 2, 0)
+    z_task(1, 0, 2, 1)
+    z_task(1, 1, 2, 1)
+    z_task(0, 0, 5, 4)
+    z_task(1, 1, 3, 2)
+    x_send(0, 4).start()
+    z_task(1, 0, 3, 2)
+    x_send(0, 3).start()
+    z_task(1, 1, 3, 0)
+    z_task(1, 0, 3, 0)
+    z_task(1, 1, 3, 1)
+    z_task(1, 0, 3, 1)
+    gate_up(0, 0, 0)
+    z_task(1, 1, 4, 2)
+    x_send(0, 6).start()
+    z_task(2, 1, 1, 2)
+    z_task(2, 1, 1, 3)
+    gate_up(0, 0, 1)
+    z_task(1, 1, 4, 0)
+    z_task(2, 1, 1, 0)
+    z_task(1, 0, 4, 2)
+    x_send(0, 5).start()
+    z_task(2, 0, 1, 2)
+    x_send(1, 0).start()
+    z_task(2, 0, 1, 3)
+    x_send_last(0).start()
+    z_task(1, 0, 4, 0)
+    z_task(2, 0, 1, 0)
+    gate_up(0, 0, 2)
+    z_task(1, 1, 4, 1)
+    z_task(2, 1, 1, 1)
+    z_task(1, 0, 4, 1)
+    z_task(2, 0, 1, 1)
+    z_task(1, 1, 5, 2)
+    x_send(0, 8).start()
+    gate_up(0, 0, 3)
+    z_task(1, 0, 5, 2)
+    x_send(0, 7).start()
+    z_task(2, 1, 2, 2)
+    x_send(1, 2).start()
+    z_task(2, 0, 2, 2)
+    x_send(1, 1).start()
+    z_task(2, 1, 2, 3)
+    x_send_last(2).start()
+    z_task(2, 0, 2, 3)
+    x_send_last(1).start()
     hidden(0, 0)
-    down(0, 0)
-    z_step(1, 5)
-    z_step(2, 2)
-    gate_up(0, 1)
+    z_task(1, 1, 5, 0)
+    z_task(1, 0, 5, 0)
+    z_task(2, 0, 2, 0)
+    z_task(2, 1, 2, 0)
+    down(0, 0, 'b')
+    z_task(1, 0, 5, 1)
+    z_task(1, 1, 5, 1)
+    gate_up(0, 1, 0)
+    down(0, 0, 'a')
+    z_task(2, 0, 2, 1)
+    gate_up(0, 1, 1)
+    z_task(2, 1, 2, 1)
+    cross(0, 4)
+    cross(0, 3)
+    gate_up(0, 1, 2)
+    gate_up(0, 1, 3)
+    z_task(2, 1, 3, 2)
+    x_send(1, 4).start()
+    z_task(2, 0, 3, 3)
+    x_send_last(3).start()
+    z_task(2, 0, 3, 2)
+    x_send(1, 3).start()
+    z_task(2, 1, 3, 3)
+    x_send_last(4).start()
+    cross(0, 1)
+    cross(0, 2)
+    cross(0, 0)
+    z_task(2, 0, 3, 0)
     hidden(0, 1)
-    z_step(2, 3)
-    down(0, 1)
-    cross(0, 7, 5, 6)
-    gate_up(1, 0)
-    z_step(2, 4)
+    z_task(2, 1, 3, 0)
+    z_task(2, 0, 3, 1)
+    down(0, 1, 'b')
+    z_task(2, 0, 4, 3)
+    x_send_last(5).start()
+    z_task(2, 1, 3, 1)
+    gate_up(1, 0, 0)
+    gate_up(1, 0, 1)
+    z_task(2, 1, 4, 2)
+    z_task(2, 0, 4, 2)
+    x_send(1, 5).start()
+    x_send(1, 6).start()
+    down(0, 1, 'a')
+    ret_task(1, 1, 1, 0)
+    z_task(2, 1, 4, 3)
+    x_send_last(6).start()
+    ret_task(1, 0, 1, 1)
+    ret_task(1, 0, 1, 0)
+    gate_up(1, 0, 2)
+    gate_up(1, 0, 3)
+    z_task(2, 0, 4, 1)
+    ret_task(1, 1, 1, 1)
+    ret_task(0, 0, 1, 4)
+    z_task(2, 1, 4, 1)
+    z_task(2, 0, 5, 3)
+    x_send_last(7).start()
+    z_task(2, 0, 4, 0)
+    ret_task(0, 1, 2, 4)
+    z_task(2, 1, 4, 0)
+    gate_up(1, 1, 0)
+    gate_up(1, 1, 1)
     hidden(1, 0)
-    ret(1, 1, 0, 1)
-    cross(0, 3, 4)
-    z_step(2, 5)
-    ret(1, 1, 2)
-    ret(1, 2, 0, 1)
-    gate_up(1, 1)
-    ret(1, 2, 2)
-    ret(1, 3, 0, 1)
-    gate_up(1, 2)
+    ret_task(1, 1, 2, 0)
+    ret_task(1, 0, 2, 0)
+    z_task(2, 0, 5, 1)
+    ret_task(1, 0, 2, 1)
+    z_task(2, 1, 5, 2)
+    x_send(1, 8).start()
+    z_task(2, 0, 5, 2)
+    x_send(1, 7).start()
+    ret_task(1, 1, 2, 1)
+    ret_task(0, 0, 2, 4)
+    down(1, 0, 'b')
+    down(1, 0, 'a')
+    ret_task(0, 1, 3, 4)
+    z_task(2, 0, 5, 0)
+    z_task(2, 1, 5, 0)
+    z_task(2, 1, 5, 1)
+    gate_up(1, 2, 0)
+    ret_task(1, 0, 3, 0)
+    gate_up(1, 2, 1)
+    ret_task(1, 1, 3, 0)
+    gate_up(1, 1, 2)
+    ret_task(1, 0, 3, 1)
+    gate_up(1, 1, 3)
+    ret_task(1, 1, 3, 1)
+    ret_task(0, 0, 3, 4)
+    ret_task(0, 1, 4, 4)
+    gate_up(1, 2, 2)
+    gate_up(1, 2, 3)
+    ret_task(1, 0, 4, 0)
     hidden(1, 1)
-    cross(0, 1, 2)
+    ret_task(1, 1, 4, 0)
+    ret_task(1, 0, 4, 1)
+    cross(0, 7)
+    cross(0, 6)
     hidden(1, 2)
-    down(1, 0)
-    ret(1, 3, 2)
-    ret(1, 4, 0, 1)
-    down(1, 2)
+    ret_task(0, 0, 4, 4)
+    ret_task(1, 1, 4, 1)
+    down(1, 1, 'b')
+    down(1, 1, 'a')
+    down(1, 2, 'b')
+    down(1, 2, 'a')
+    ret_task(2, 0, 1, 1)
+    ret_task(2, 1, 1, 0)
+    ret_task(1, 0, 1, 2)
+    ret_task(2, 0, 1, 0)
+    ret_task(0, 0, 1, 2)
+    finish(0, 4)
+    ret_task(2, 1, 1, 1)
+    finish(1, 0)
+    finish(1, 1)
+    ret_task(1, 1, 1, 2)
+    ret_task(2, 0, 2, 1)
+    ret_task(2, 1, 2, 0)
     cross(1, 7)
-    ret(2, 1, 0, 1)
-    cross(0, 0)
-    down(1, 1)
-    cross(1, 5, 6)
-    ret(1, 4, 2)
-    ret(2, 2, 0, 1)
-    ret(2, 1, 3, 2)
-    finish(1, 0, 1)
-    cross(1, 3, 4)
-    ret(0, 1, 4)
-    ret(2, 3, 0, 1)
-    ret(2, 2, 3, 2)
-    ret(0, 1, 2)
-    ret(0, 2, 4)
-    finish(1, 2)
-    cross(1, 1, 2, 0)
+    hand_out(0, 0)
+    cross(1, 5)
+    ret_task(2, 0, 2, 0)
+    ret_task(2, 1, 2, 1)
+    cross(1, 6)
+    cross(1, 3)
+    cross(1, 4)
+    cross(0, 5)
     hand_out(1, 0)
-    hand_out(1, 1)
-    ret(2, 4, 0, 1)
-    ret(2, 3, 3, 2)
-    ret(0, 2, 2)
-    ret(0, 3, 4)
-    finish(2, 0, 1)
-    ret(2, 4, 3, 2)
-    ret(0, 3, 2)
-    ret(0, 4, 4)
+    cross(1, 1)
+    cross(1, 2)
+    cross(1, 0)
+    ret_task(2, 0, 3, 1)
+    ret_task(2, 1, 3, 0)
+    ret_task(2, 0, 1, 3)
+    ret_task(2, 0, 1, 2)
+    ret_task(2, 1, 1, 2)
+    ret_task(2, 0, 3, 0)
+    ret_task(2, 1, 3, 1)
+    ret_task(2, 0, 4, 1)
+    ret_task(2, 1, 4, 0)
+    ret_task(2, 0, 2, 3)
+    ret_task(2, 1, 2, 3)
+    ret_task(2, 1, 2, 2)
+    ret_task(2, 0, 2, 2)
+    ret_task(2, 1, 4, 1)
+    ret_task(2, 0, 4, 0)
+    ret_task(2, 1, 3, 3)
+    ret_task(2, 0, 3, 3)
+    ret_task(1, 1, 2, 2)
+    ret_task(1, 0, 2, 2)
+    ret_task(2, 0, 3, 2)
+    ret_task(0, 0, 2, 2)
+    ret_task(2, 1, 3, 2)
+    ret_task(0, 1, 2, 2)
+    finish(2, 0)
+    finish(2, 1)
+    ret_task(2, 1, 4, 3)
+    ret_task(2, 0, 4, 3)
+    ret_task(1, 0, 3, 2)
+    ret_task(1, 1, 3, 2)
+    ret_task(2, 1, 4, 2)
+    ret_task(2, 0, 4, 2)
+    ret_task(0, 1, 3, 2)
+    ret_task(0, 0, 3, 2)
+    finish(2, 3)
     hand_out(2, 0)
-    finish(2, 3)
+    ret_task(1, 1, 4, 2)
+    ret_task(1, 0, 4, 2)
+    hand_out_last()
     finish(2, 2)
     hand_out(2, 1)
-    ret(0, 4, 2)
-    hand_out_last()
-    finish(0, 4, 2)
-    hand_out(0, 0)
+    ret_task(0, 0, 4, 2)
+    ret_task(0, 1, 4, 2)
+    finish(1, 2)
+    hand_out(1, 1)
+    finish(0, 2)
     hand_out(0, 1)
+
     seven = pl.ds(0, 7)
     wait_for(as_sem.at[0], send.at[seven])
     wait_for(as_sem.at[1], send_x.at[seven])

time: 129 us -> 122 us (0.946)
  Pallas kernels: 127 us -> 120 us
    pallas_call x1, Pallas kernels: 127 us -> 120 us  [local(): pl.pallas_call(kernel, out_shape=jax.ShapeDtypeStruct((n_tok, wa + wb), B...]
where the time goes in v5:
time: 122 us
  Pallas kernels  120 us (98%)
  local copies, waits for them, and re-layouts  1.77 us (1%)
    pallas_call x1, Pallas kernels, local(): pl.pallas_call(kernel, out_shape=jax.ShapeDtypeStruct((n_tok, wa + wb), B...  120 us

profile of v5, /device:TPU:6, one launch (start us, length us, event | category | flops | bytes accessed | tf_op | source)
XLA Modules:
  0.0 121.7 jit_solution(16208796760699736601)
XLA Ops:
  0.0 119.9 %routed_experts.1 = bf16[128,1536]{1,0:T(8,128)(2,1)} custom-call(bf16[128,6144]{1,0:T(8,128)(2,1)} %tok_ref.1, s32[1,128]{1,0:T(1,128)} %bitcast.2, f32[1,128]{1,0:T(1,128)} %bitcast.3, bf16[168,6144]{1,0:T(8,128)(2,1)} %wg_ref.1, bf16[168,6144]{1,0:T(8,128)(2,1)} %wu_ref.1, bf16[168,6144]{1,0:T(8,128)(2,1)} %wd_ref.1), custom_call_target="tpu_custom_call" | custom-call | flops 7000000000 | bytes 10000000 | tf_op jit(solution)/shard_map/routed_experts/pallas_call | solution.py:786
  119.9 1.8 %copy.8 = bf16[128,1536]{1,0:T(8,128)(2,1)} copy(bf16[128,1536]{1,0:T(8,128)(2,1)} %routed_experts.1) | data formatting | bytes 786432

commit v6 on v5

--- a/solution.py
+++ b/solution.py
@@ -485,260 +485,260 @@
         for r in range(1, EXPERTS):
             phase_a_last(r).start()
 
+    z_task(0, 1, 1, 4)
     z_task(0, 0, 1, 2)
+    z_task(0, 0, 1, 4)
     z_task(0, 1, 1, 2)
-    z_task(0, 1, 1, 4)
-    z_task(0, 0, 1, 4)
-    start_rest()
     z_task(0, 0, 2, 2)
-    z_task(0, 1, 2, 2)
     z_task(0, 0, 2, 4)
     z_task(0, 1, 2, 4)
     z_task(0, 0, 3, 2)
+    z_task(0, 1, 2, 2)
+    start_rest()
+    z_task(0, 1, 3, 4)
+    z_task(0, 0, 3, 4)
+    z_task(0, 0, 4, 2)
     z_task(0, 1, 3, 2)
-    z_task(0, 0, 3, 4)
-    z_task(0, 1, 3, 4)
-    z_task(0, 0, 4, 2)
-    z_task(0, 1, 4, 2)
     land(0)
+    z_task(1, 0, 1, 0)
+    z_task(1, 1, 1, 1)
     z_task(1, 0, 1, 2)
     z_task(1, 1, 1, 2)
-    x_send(0, 0).start()
     z_task(1, 1, 1, 0)
-    z_task(1, 0, 1, 0)
-    z_task(1, 0, 1, 1)
-    z_task(0, 0, 4, 4)
-    z_task(1, 1, 1, 1)
-    z_task(0, 1, 4, 4)
-    z_task(0, 0, 5, 2)
     land(1)
     land_last()
+    x_send(0, 0).start()
     weights_wait(w_sem)
     weights_wait(wr_sem)
+    z_task(1, 0, 1, 1)
+    z_task(2, 0, 1, 2)
+    z_task(1, 1, 2, 1)
+    z_task(1, 1, 2, 2)
     z_task(1, 0, 2, 2)
+    z_task(1, 0, 2, 1)
+    z_task(1, 1, 2, 0)
+    z_task(2, 0, 1, 3)
+    z_task(0, 1, 4, 4)
+    z_task(1, 1, 3, 1)
+    z_task(0, 1, 4, 2)
+    z_task(2, 1, 1, 3)
+    z_task(1, 1, 3, 2)
+    x_send(0, 2).start()
+    z_task(1, 0, 3, 2)
+    z_task(2, 1, 1, 2)
     x_send(0, 1).start()
-    z_task(1, 1, 2, 2)
-    x_send(0, 2).start()
+    z_task(1, 1, 3, 0)
+    x_send(0, 4).start()
     z_task(1, 0, 2, 0)
-    z_task(1, 1, 2, 0)
-    z_task(1, 0, 2, 1)
-    z_task(1, 1, 2, 1)
-    z_task(0, 0, 5, 4)
-    z_task(1, 1, 3, 2)
-    x_send(0, 4).start()
-    z_task(1, 0, 3, 2)
     x_send(0, 3).start()
-    z_task(1, 1, 3, 0)
+    z_task(1, 0, 3, 1)
+    z_task(0, 0, 5, 2)
+    z_task(2, 1, 2, 3)
+    z_task(2, 0, 2, 3)
+    z_task(1, 0, 4, 2)
     z_task(1, 0, 3, 0)
-    z_task(1, 1, 3, 1)
-    z_task(1, 0, 3, 1)
     gate_up(0, 0, 0)
     z_task(1, 1, 4, 2)
+    z_task(1, 0, 4, 1)
+    x_send(0, 5).start()
+    z_task(0, 0, 4, 4)
+    gate_up(0, 0, 1)
+    z_task(2, 0, 3, 3)
+    z_task(2, 1, 2, 2)
+    z_task(1, 0, 5, 2)
+    z_task(1, 1, 4, 1)
+    z_task(1, 1, 4, 0)
+    z_task(2, 0, 2, 2)
     x_send(0, 6).start()
-    z_task(2, 1, 1, 2)
-    z_task(2, 1, 1, 3)
-    gate_up(0, 0, 1)
-    z_task(1, 1, 4, 0)
+    gate_up(0, 0, 2)
+    z_task(2, 1, 1, 1)
+    gate_up(0, 0, 3)
     z_task(2, 1, 1, 0)
-    z_task(1, 0, 4, 2)
-    x_send(0, 5).start()
-    z_task(2, 0, 1, 2)
+    x_send(0, 7).start()
+    z_task(1, 0, 4, 0)
+    z_task(2, 0, 1, 1)
+    z_task(1, 1, 5, 1)
+    z_task(1, 1, 5, 2)
+    z_task(1, 0, 5, 1)
+    x_send(0, 8).start()
+    x_send_last(1).start()
     x_send(1, 0).start()
-    z_task(2, 0, 1, 3)
-    x_send_last(0).start()
-    z_task(1, 0, 4, 0)
+    z_task(2, 0, 4, 3)
     z_task(2, 0, 1, 0)
-    gate_up(0, 0, 2)
-    z_task(1, 1, 4, 1)
-    z_task(2, 1, 1, 1)
-    z_task(1, 0, 4, 1)
-    z_task(2, 0, 1, 1)
-    z_task(1, 1, 5, 2)
-    x_send(0, 8).start()
-    gate_up(0, 0, 3)
-    z_task(1, 0, 5, 2)
-    x_send(0, 7).start()
-    z_task(2, 1, 2, 2)
-    x_send(1, 2).start()
-    z_task(2, 0, 2, 2)
+    z_task(2, 0, 3, 2)
+    z_task(0, 0, 5, 4)
+    z_task(1, 0, 5, 0)
     x_send(1, 1).start()
-    z_task(2, 1, 2, 3)
-    x_send_last(2).start()
-    z_task(2, 0, 2, 3)
-    x_send_last(1).start()
+    z_task(2, 1, 3, 2)
     hidden(0, 0)
     z_task(1, 1, 5, 0)
-    z_task(1, 0, 5, 0)
-    z_task(2, 0, 2, 0)
+    x_send_last(5).start()
+    gate_up(0, 1, 0)
+    gate_up(0, 1, 1)
+    gate_up(0, 1, 2)
+    z_task(2, 0, 5, 3)
+    z_task(2, 1, 3, 3)
+    x_send(1, 2).start()
+    gate_up(0, 1, 3)
+    z_task(2, 0, 2, 1)
     z_task(2, 1, 2, 0)
     down(0, 0, 'b')
-    z_task(1, 0, 5, 1)
-    z_task(1, 1, 5, 1)
-    gate_up(0, 1, 0)
+    z_task(2, 1, 2, 1)
+    z_task(2, 1, 4, 2)
+    z_task(2, 0, 2, 0)
+    x_send(1, 6).start()
+    x_send_last(2).start()
+    z_task(2, 1, 4, 3)
+    hidden(0, 1)
     down(0, 0, 'a')
-    z_task(2, 0, 2, 1)
-    gate_up(0, 1, 1)
-    z_task(2, 1, 2, 1)
-    cross(0, 4)
-    cross(0, 3)
-    gate_up(0, 1, 2)
-    gate_up(0, 1, 3)
-    z_task(2, 1, 3, 2)
-    x_send(1, 4).start()
-    z_task(2, 0, 3, 3)
-    x_send_last(3).start()
-    z_task(2, 0, 3, 2)
-    x_send(1, 3).start()
-    z_task(2, 1, 3, 3)
-    x_send_last(4).start()
-    cross(0, 1)
-    cross(0, 2)
-    cross(0, 0)
-    z_task(2, 0, 3, 0)
-    hidden(0, 1)
-    z_task(2, 1, 3, 0)
-    z_task(2, 0, 3, 1)
-    down(0, 1, 'b')
-    z_task(2, 0, 4, 3)
-    x_send_last(5).start()
-    z_task(2, 1, 3, 1)
-    gate_up(1, 0, 0)
-    gate_up(1, 0, 1)
-    z_task(2, 1, 4, 2)
     z_task(2, 0, 4, 2)
     x_send(1, 5).start()
-    x_send(1, 6).start()
+    x_send(1, 4).start()
+    x_send_last(3).start()
+    down(0, 1, 'b')
+    z_task(2, 0, 3, 1)
+    x_send_last(6).start()
+    z_task(2, 1, 3, 0)
     down(0, 1, 'a')
+    x_send_last(7).start()
+    z_task(2, 1, 3, 1)
+    z_task(2, 0, 3, 0)
+    cross(0, 6)
     ret_task(1, 1, 1, 0)
-    z_task(2, 1, 4, 3)
-    x_send_last(6).start()
+    ret_task(1, 0, 1, 0)
     ret_task(1, 0, 1, 1)
-    ret_task(1, 0, 1, 0)
-    gate_up(1, 0, 2)
-    gate_up(1, 0, 3)
+    ret_task(0, 0, 1, 4)
+    cross(0, 7)
+    x_send_last(0).start()
+    x_send_last(4).start()
+    gate_up(1, 0, 0)
+    z_task(2, 0, 5, 2)
+    x_send(1, 7).start()
+    z_task(2, 1, 5, 2)
+    z_task(2, 1, 4, 0)
     z_task(2, 0, 4, 1)
+    x_send(1, 8).start()
+    gate_up(1, 0, 1)
+    cross(0, 5)
     ret_task(1, 1, 1, 1)
-    ret_task(0, 0, 1, 4)
+    cross(0, 1)
+    x_send(1, 3).start()
     z_task(2, 1, 4, 1)
-    z_task(2, 0, 5, 3)
-    x_send_last(7).start()
     z_task(2, 0, 4, 0)
-    ret_task(0, 1, 2, 4)
-    z_task(2, 1, 4, 0)
     gate_up(1, 1, 0)
     gate_up(1, 1, 1)
+    ret_task(0, 1, 2, 4)
+    ret_task(1, 0, 2, 1)
+    ret_task(1, 0, 2, 0)
+    z_task(2, 1, 5, 0)
+    gate_up(1, 1, 2)
+    ret_task(1, 1, 2, 0)
+    gate_up(1, 1, 3)
+    ret_task(1, 0, 1, 2)
+    ret_task(1, 1, 2, 1)
+    z_task(2, 0, 5, 0)
+    z_task(2, 1, 5, 1)
+    z_task(2, 0, 5, 1)
+    gate_up(1, 2, 0)
+    gate_up(1, 2, 1)
+    ret_task(1, 0, 3, 1)
+    ret_task(1, 1, 1, 2)
+    ret_task(0, 0, 2, 4)
+    gate_up(1, 2, 2)
+    ret_task(0, 0, 1, 2)
+    ret_task(1, 1, 3, 0)
+    cross(0, 4)
+    gate_up(1, 2, 3)
+    ret_task(1, 0, 3, 0)
+    hidden(1, 1)
+    ret_task(1, 0, 2, 2)
+    ret_task(1, 1, 3, 1)
+    ret_task(1, 0, 4, 1)
+    hidden(1, 2)
+    ret_task(1, 1, 2, 2)
+    down(1, 1, 'b')
+    ret_task(0, 0, 3, 4)
+    ret_task(0, 1, 3, 4)
+    down(1, 2, 'b')
+    down(1, 2, 'a')
+    ret_task(1, 1, 4, 0)
+    cross(1, 7)
+    ret_task(2, 0, 1, 0)
+    gate_up(1, 0, 2)
+    ret_task(2, 1, 1, 1)
+    cross(1, 5)
+    ret_task(1, 1, 4, 1)
+    ret_task(1, 0, 4, 0)
+    gate_up(1, 0, 3)
+    ret_task(2, 0, 1, 1)
+    ret_task(2, 1, 1, 0)
+    down(1, 1, 'a')
+    ret_task(2, 0, 1, 3)
+    cross(1, 6)
+    ret_task(2, 1, 1, 2)
+    ret_task(2, 0, 2, 0)
     hidden(1, 0)
-    ret_task(1, 1, 2, 0)
-    ret_task(1, 0, 2, 0)
-    z_task(2, 0, 5, 1)
-    ret_task(1, 0, 2, 1)
-    z_task(2, 1, 5, 2)
-    x_send(1, 8).start()
-    z_task(2, 0, 5, 2)
-    x_send(1, 7).start()
-    ret_task(1, 1, 2, 1)
-    ret_task(0, 0, 2, 4)
+    ret_task(0, 1, 2, 2)
+    ret_task(2, 1, 2, 1)
+    ret_task(2, 0, 1, 2)
+    cross(0, 3)
+    ret_task(2, 0, 2, 1)
+    cross(0, 2)
+    ret_task(2, 1, 2, 0)
     down(1, 0, 'b')
     down(1, 0, 'a')
-    ret_task(0, 1, 3, 4)
-    z_task(2, 0, 5, 0)
-    z_task(2, 1, 5, 0)
-    z_task(2, 1, 5, 1)
-    gate_up(1, 2, 0)
-    ret_task(1, 0, 3, 0)
-    gate_up(1, 2, 1)
-    ret_task(1, 1, 3, 0)
-    gate_up(1, 1, 2)
-    ret_task(1, 0, 3, 1)
-    gate_up(1, 1, 3)
-    ret_task(1, 1, 3, 1)
-    ret_task(0, 0, 3, 4)
-    ret_task(0, 1, 4, 4)
-    gate_up(1, 2, 2)
-    gate_up(1, 2, 3)
-    ret_task(1, 0, 4, 0)
-    hidden(1, 1)
-    ret_task(1, 1, 4, 0)
-    ret_task(1, 0, 4, 1)
-    cross(0, 7)
-    cross(0, 6)
-    hidden(1, 2)
-    ret_task(0, 0, 4, 4)
-    ret_task(1, 1, 4, 1)
-    down(1, 1, 'b')
-    down(1, 1, 'a')
-    down(1, 2, 'b')
-    down(1, 2, 'a')
-    ret_task(2, 0, 1, 1)
-    ret_task(2, 1, 1, 0)
-    ret_task(1, 0, 1, 2)
-    ret_task(2, 0, 1, 0)
-    ret_task(0, 0, 1, 2)
-    finish(0, 4)
-    ret_task(2, 1, 1, 1)
-    finish(1, 0)
-    finish(1, 1)
-    ret_task(1, 1, 1, 2)
-    ret_task(2, 0, 2, 1)
-    ret_task(2, 1, 2, 0)
-    cross(1, 7)
-    hand_out(0, 0)
-    cross(1, 5)
-    ret_task(2, 0, 2, 0)
-    ret_task(2, 1, 2, 1)
-    cross(1, 6)
-    cross(1, 3)
+    ret_task(2, 0, 3, 0)
+    ret_task(2, 0, 2, 2)
+    ret_task(2, 1, 2, 3)
     cross(1, 4)
-    cross(0, 5)
-    hand_out(1, 0)
-    cross(1, 1)
-    cross(1, 2)
-    cross(1, 0)
+    ret_task(2, 1, 3, 1)
     ret_task(2, 0, 3, 1)
     ret_task(2, 1, 3, 0)
-    ret_task(2, 0, 1, 3)
-    ret_task(2, 0, 1, 2)
-    ret_task(2, 1, 1, 2)
-    ret_task(2, 0, 3, 0)
-    ret_task(2, 1, 3, 1)
+    cross(1, 2)
+    ret_task(2, 0, 4, 0)
+    finish(1, 0)
+    ret_task(2, 1, 2, 2)
+    ret_task(2, 0, 2, 3)
+    cross(1, 3)
+    finish(1, 1)
+    ret_task(2, 1, 4, 0)
     ret_task(2, 0, 4, 1)
-    ret_task(2, 1, 4, 0)
-    ret_task(2, 0, 2, 3)
-    ret_task(2, 1, 2, 3)
-    ret_task(2, 1, 2, 2)
-    ret_task(2, 0, 2, 2)
     ret_task(2, 1, 4, 1)
-    ret_task(2, 0, 4, 0)
+    cross(1, 1)
     ret_task(2, 1, 3, 3)
+    ret_task(1, 1, 3, 2)
+    ret_task(2, 1, 3, 2)
+    cross(1, 0)
     ret_task(2, 0, 3, 3)
-    ret_task(1, 1, 2, 2)
-    ret_task(1, 0, 2, 2)
+    ret_task(1, 0, 3, 2)
     ret_task(2, 0, 3, 2)
-    ret_task(0, 0, 2, 2)
-    ret_task(2, 1, 3, 2)
-    ret_task(0, 1, 2, 2)
     finish(2, 0)
     finish(2, 1)
+    ret_task(2, 0, 4, 3)
+    cross(0, 0)
+    hand_out(1, 0)
     ret_task(2, 1, 4, 3)
-    ret_task(2, 0, 4, 3)
-    ret_task(1, 0, 3, 2)
-    ret_task(1, 1, 3, 2)
+    ret_task(1, 0, 4, 2)
+    ret_task(0, 0, 2, 2)
+    ret_task(1, 1, 4, 2)
+    ret_task(2, 0, 4, 2)
     ret_task(2, 1, 4, 2)
-    ret_task(2, 0, 4, 2)
+    hand_out(2, 0)
     ret_task(0, 1, 3, 2)
+    ret_task(0, 0, 4, 4)
+    finish(2, 3)
+    finish(1, 2)
+    hand_out(1, 1)
     ret_task(0, 0, 3, 2)
-    finish(2, 3)
-    hand_out(2, 0)
-    ret_task(1, 1, 4, 2)
-    ret_task(1, 0, 4, 2)
+    ret_task(0, 1, 4, 4)
     hand_out_last()
     finish(2, 2)
     hand_out(2, 1)
     ret_task(0, 0, 4, 2)
+    finish(0, 4)
     ret_task(0, 1, 4, 2)
-    finish(1, 2)
-    hand_out(1, 1)
     finish(0, 2)
+    hand_out(0, 0)
     hand_out(0, 1)
 
     seven = pl.ds(0, 7)

time: 122 us -> 120 us (0.984)
  Pallas kernels: 120 us -> 117 us
    pallas_call x1, Pallas kernels: 120 us -> 117 us  [local(): pl.pallas_call(kernel, out_shape=jax.ShapeDtypeStruct((n_tok, wa + wb), B...]
where the time goes in v6:
time: 120 us; the launch traced here: 119 us
  Pallas kernels  117 us (98%)
  local copies, waits for them, and re-layouts  1.77 us (1%)
    pallas_call x1, Pallas kernels, local(): pl.pallas_call(kernel, out_shape=jax.ShapeDtypeStruct((n_tok, wa + wb), B...  117 us

profile of v6, /device:TPU:6, one launch (start us, length us, event | category | flops | bytes accessed | tf_op | source)
XLA Modules:
  0.0 118.8 jit_solution(6068833673113491335)
XLA Ops:
  0.0 117.0 %routed_experts.1 = bf16[128,1536]{1,0:T(8,128)(2,1)} custom-call(bf16[128,6144]{1,0:T(8,128)(2,1)} %tok_ref.1, s32[1,128]{1,0:T(1,128)} %bitcast.2, f32[1,128]{1,0:T(1,128)} %bitcast.3, bf16[168,6144]{1,0:T(8,128)(2,1)} %wg_ref.1, bf16[168,6144]{1,0:T(8,128)(2,1)} %wu_ref.1, bf16[168,6144]{1,0:T(8,128)(2,1)} %wd_ref.1), custom_call_target="tpu_custom_call" | custom-call | flops 7000000000 | bytes 10000000 | tf_op jit(solution)/shard_map/routed_experts/pallas_call | solution.py:786
  117.0 1.8 %copy.8 = bf16[128,1536]{1,0:T(8,128)(2,1)} copy(bf16[128,1536]{1,0:T(8,128)(2,1)} %routed_experts.1) | data formatting | bytes 786432

commit v7 on v4

--- a/solution.py
+++ b/solution.py
@@ -13,7 +13,7 @@
 RING = 8
 N = 4 * MAIN
 BF16, F32 = jnp.bfloat16, jnp.float32
-SOURCES = ((0, 0), (0, 2), (1, 0), (1, 2), (0, 1), (0, 3), (1, 1), (1, 3))
+SOURCES = ((0, 0), (0, 1), (0, 3), (1, 0), (0, 2), (1, 1), (1, 3), (1, 2))
 UNITS = (
     (0, 0, 16, (2, 4), ((0, 16), (0, 16))),
     (0, 16, 48, (2, 0, 1), ((16, 16), (32, 32))),
@@ -88,7 +88,7 @@
     if k < 4:
         return True
     if u == 0:
-        return side == (0 if p == 2 else 1)
+        return side == 0
     return p != 3 or side == 0
 
 
@@ -273,18 +273,11 @@
         blk = xo.at[plane(ORDER[i]), xl, :, wa:]
         return remote(blk, blk, xs_sem.at[2], xr_sem.at[2, group_of(1, i)], across)
 
-    def z_step(u, k):
-        w = UNITS[u][0]
-        for p in UNITS[u][3]:
-            for side in range(2):
-                if k > 1 and moves(u, side, k - 1, p):
-                    z_send(u, side, k - 1, p).wait_recv()
-                if k < 5 and moves(u, side, k, p):
-                    z_send(u, side, k, p).start()
-                if u and p == 2 and (k > 1 or side == 0):
-                    x_send(w, 2 * (k - 1) - 1 + side if k > 1 else 0).start()
-                if p == 3 and not (k in (1, 5) and side == 1):
-                    x_send_last(2 * (k - 1) - 1 + side if k > 1 else 0).start()
+    def z_task(u, side, k, p):
+        if k > 1 and moves(u, side, k - 1, p):
+            z_send(u, side, k - 1, p).wait_recv()
+        if k < 5 and moves(u, side, k, p):
+            z_send(u, side, k, p).start()
 
     def gu_send(w, g):
         lo, n, _ = group_rows(w, g)
@@ -302,26 +295,27 @@
         both = xo[pi, blk - 2, :, wa:].astype(F32)
         return jnp.concatenate([both[:8], both[8:, :wb - wo]], axis=1)
 
-    def gate_up(w, g):
+    def gate_up(w, g, blk):
         lo, n, extra = group_rows(w, g)
         ids = range(*GROUPS[w][g])
-        wait_for(xr_sem.at[w, g], yx[w].at[pl.ds(0, len(ids))])
-        if w == 1:
-            wait_for(xr_sem.at[2, g], yxo.at[pl.ds(0, len(ids))])
-        for blk in range(4):
-            xs, wgu = (x_b[w], wgu_b) if blk >= 2 else (x_a[w], wgu_a)
-            parts = [xs[plane(ORDER[i]), blk % 2] for i in ids]
-            if extra:
-                lasts = [last_rows(plane(ORDER[i]), blk) for i in ids]
-                if len(lasts) % 2:
-                    lasts.append(jnp.zeros_like(lasts[0]))
-                parts.append(jnp.concatenate(lasts, axis=0).astype(BF16))
-            rows = jnp.concatenate(parts, axis=0)
-            for m in range(2):
-                for acc, u in ((gu_own[w], co), (gu_out[w], 1 - co)):
-                    term = nt_dot(rows, wgu[m, u, blk % 2])
-                    acc[m, lo:lo + n] = acc[m, lo:lo + n] + term if blk else term
-        gu_send(w, g).start()
+        if blk == 2:
+            wait_for(xr_sem.at[w, g], yx[w].at[pl.ds(0, len(ids))])
+            if w == 1:
+                wait_for(xr_sem.at[2, g], yxo.at[pl.ds(0, len(ids))])
+        xs, wgu = (x_b[w], wgu_b) if blk >= 2 else (x_a[w], wgu_a)
+        parts = [xs[plane(ORDER[i]), blk % 2] for i in ids]
+        if extra:
+            lasts = [last_rows(plane(ORDER[i]), blk) for i in ids]
+            if len(lasts) % 2:
+                lasts.append(jnp.zeros_like(lasts[0]))
+            parts.append(jnp.concatenate(lasts, axis=0).astype(BF16))
+        rows = jnp.concatenate(parts, axis=0)
+        for m in range(2):
+            for acc, u in ((gu_own[w], co), (gu_out[w], 1 - co)):
+                term = nt_dot(rows, wgu[m, u, blk % 2])
+                acc[m, lo:lo + n] = acc[m, lo:lo + n] + term if blk else term
+        if blk == 3:
+            gu_send(w, g).start()
 
     def hidden(w, g):
         lo, n, _ = group_rows(w, g)
@@ -331,12 +325,13 @@
         hid[w][co, lo:lo + n] = (gate / (1.0 + jnp.exp(-gate)) * up).astype(BF16)
         hid_send(w, g).start()
 
-    def down(w, g):
+    def down(w, g, kind):
         lo, n, extra = group_rows(w, g)
         ids = range(*GROUPS[w][g])
-        hid_send(w, g).wait_recv()
+        if kind == "b":
+            hid_send(w, g).wait_recv()
         lasts = {}
-        for blk in (2, 3, 0, 1):
+        for blk in ((2, 3) if kind == "b" else (0, 1)):
             wdn, ys = (wdn_b, y_b[w]) if blk >= 2 else (wdn_a, y_a[w])
             part = dot(hid[w][0, lo:lo + n], wdn[0, blk % 2]) + dot(hid[w][1, lo:lo + n], wdn[1, blk % 2])
             for at, i in enumerate(ids):
@@ -400,20 +395,15 @@
         here = block(y_all, w, plane(d * (5 - j)), p, rows_of(u, side, 5 - j))
         return remote(here, back_block(u, side, j, p), sent(bs_sem, w, p), lane(br_sems, u, side, j, p), on_z(d))
 
-    def ret(u, j, *ps):
-        w = UNITS[u][0]
-        for p in ps:
-            for side in range(2):
-                if not moves(u, side, 5 - j, p):
-                    continue
-                d = 1 - 2 * side
-                if p in (2, 3):
-                    add_across(w, p, 5 - j)
-                if j > 1 and moves(u, side, 6 - j, p):
-                    back_send(u, side, j - 1, p).wait_recv()
-                    here = block(y_all, w, plane(d * (5 - j)), p, rows_of(u, side, 6 - j))
-                    here[...] = (here[...].astype(F32) + back_block(u, side, j - 1, p)[...].astype(F32)).astype(BF16)
-                back_send(u, side, j, p).start()
+    def ret_task(u, side, j, p):
+        w, d = UNITS[u][0], 1 - 2 * side
+        if p in (2, 3):
+            add_across(w, p, 5 - j)
+        if j > 1 and moves(u, side, 6 - j, p):
+            back_send(u, side, j - 1, p).wait_recv()
+            here = block(y_all, w, plane(d * (5 - j)), p, rows_of(u, side, 6 - j))
+            here[...] = (here[...].astype(F32) + back_block(u, side, j - 1, p)[...].astype(F32)).astype(BF16)
+        back_send(u, side, j, p).start()
 
     def f_send(u):
         w, lo, n = UNITS[u][:3]
@@ -495,87 +485,262 @@
         for r in range(1, EXPERTS):
             phase_a_last(r).start()
 
-    z_step(0, 1)
+    z_task(0, 0, 1, 4)
+    z_task(0, 0, 1, 2)
+    z_task(0, 1, 1, 2)
+    z_task(0, 1, 1, 4)
     start_rest()
-    z_step(0, 2)
-    z_step(0, 3)
+    z_task(0, 1, 2, 2)
+    z_task(0, 0, 2, 4)
+    z_task(0, 1, 2, 4)
+    z_task(0, 0, 2, 2)
+    z_task(0, 0, 3, 4)
+    z_task(0, 1, 3, 2)
+    z_task(0, 1, 3, 4)
+    z_task(0, 0, 3, 2)
     land(0)
-    z_step(1, 1)
-    z_step(0, 4)
-    z_step(0, 5)
+    z_task(1, 0, 1, 1)
+    z_task(1, 0, 1, 0)
+    z_task(1, 1, 1, 2)
+    z_task(1, 1, 1, 1)
+    z_task(1, 1, 1, 0)
+    z_task(1, 0, 1, 2)
+    z_task(1, 1, 2, 2)
+    x_send(0, 2).start()
+    z_task(1, 0, 2, 1)
+    z_task(0, 0, 4, 2)
     land(1)
     land_last()
+    z_task(2, 1, 1, 3)
+    z_task(1, 0, 2, 2)
+    z_task(1, 0, 2, 0)
+    x_send(0, 1).start()
+    z_task(0, 1, 4, 2)
+    z_task(1, 1, 2, 1)
+    z_task(1, 1, 2, 0)
+    z_task(2, 0, 1, 3)
+    x_send(0, 0).start()
+    z_task(2, 1, 1, 2)
+    z_task(1, 0, 3, 2)
+    z_task(1, 1, 3, 2)
+    x_send(0, 3).start()
+    z_task(1, 0, 3, 1)
+    z_task(1, 0, 3, 0)
+    z_task(1, 1, 3, 1)
+    x_send(0, 4).start()
+    z_task(0, 1, 4, 4)
+    z_task(2, 0, 1, 2)
+    z_task(1, 1, 3, 0)
+    z_task(0, 0, 4, 4)
+    z_task(1, 1, 4, 2)
     weights_wait(w_sem)
     weights_wait(wr_sem)
-    z_step(1, 2)
-    z_step(1, 3)
-    gate_up(0, 0)
-    z_step(1, 4)
-    z_step(2, 1)
+    x_send(1, 0).start()
+    x_send(0, 6).start()
+    z_task(0, 0, 5, 2)
+    gate_up(0, 0, 0)
+    z_task(1, 1, 4, 1)
+    z_task(1, 0, 4, 2)
+    z_task(1, 0, 4, 1)
+    gate_up(0, 0, 1)
+    z_task(2, 1, 2, 2)
+    z_task(1, 0, 4, 0)
+    z_task(2, 0, 1, 0)
+    gate_up(0, 0, 2)
+    z_task(2, 0, 2, 3)
+    z_task(1, 1, 4, 0)
+    z_task(1, 1, 5, 2)
+    x_send(0, 5).start()
+    z_task(2, 0, 2, 2)
+    gate_up(0, 0, 3)
+    z_task(2, 1, 1, 1)
+    z_task(1, 1, 5, 1)
+    x_send(0, 8).start()
+    z_task(1, 0, 5, 2)
+    z_task(2, 0, 1, 1)
+    z_task(2, 1, 2, 3)
+    x_send(0, 7).start()
+    z_task(2, 1, 1, 0)
     hidden(0, 0)
-    down(0, 0)
-    z_step(1, 5)
-    z_step(2, 2)
-    gate_up(0, 1)
+    x_send(1, 2).start()
+    z_task(1, 0, 5, 0)
+    z_task(2, 0, 2, 0)
+    z_task(0, 0, 5, 4)
+    z_task(1, 1, 5, 0)
+    z_task(2, 1, 3, 2)
+    x_send(1, 1).start()
+    z_task(2, 0, 3, 3)
+    z_task(1, 0, 5, 1)
+    x_send(1, 4).start()
+    gate_up(0, 1, 0)
+    gate_up(0, 1, 1)
+    gate_up(0, 1, 2)
+    z_task(2, 1, 2, 1)
+    gate_up(0, 1, 3)
+    z_task(2, 1, 3, 3)
+    x_send_last(3).start()
+    x_send_last(4).start()
+    x_send_last(0).start()
+    z_task(2, 0, 2, 1)
+    down(0, 0, 'b')
+    down(0, 0, 'a')
+    z_task(2, 0, 3, 2)
+    z_task(2, 1, 2, 0)
+    x_send_last(2).start()
+    x_send_last(1).start()
     hidden(0, 1)
-    z_step(2, 3)
-    down(0, 1)
-    cross(0, 7, 5, 6)
-    gate_up(1, 0)
-    z_step(2, 4)
+    z_task(2, 0, 4, 3)
+    z_task(2, 1, 4, 2)
+    x_send(1, 6).start()
+    x_send(1, 3).start()
+    z_task(2, 0, 3, 1)
+    z_task(2, 1, 3, 1)
+    down(0, 1, 'b')
+    cross(0, 6)
+    down(0, 1, 'a')
+    ret_task(1, 1, 1, 0)
+    z_task(2, 0, 3, 0)
+    z_task(2, 1, 3, 0)
+    ret_task(1, 1, 1, 1)
+    gate_up(1, 0, 0)
+    cross(0, 5)
+    ret_task(1, 0, 1, 1)
+    z_task(2, 1, 5, 2)
+    gate_up(1, 0, 1)
+    cross(0, 7)
+    z_task(2, 0, 5, 3)
+    ret_task(1, 0, 1, 0)
+    z_task(2, 1, 4, 3)
+    z_task(2, 0, 4, 2)
+    gate_up(1, 0, 2)
+    x_send_last(5).start()
+    x_send_last(7).start()
+    z_task(2, 0, 4, 0)
+    ret_task(0, 0, 1, 4)
+    ret_task(1, 1, 2, 0)
+    z_task(2, 1, 4, 1)
+    gate_up(1, 0, 3)
+    z_task(2, 1, 4, 0)
+    ret_task(1, 0, 2, 0)
+    z_task(2, 0, 5, 2)
+    x_send(1, 8).start()
+    z_task(2, 0, 4, 1)
+    ret_task(1, 1, 2, 1)
+    cross(0, 1)
+    gate_up(1, 1, 0)
+    ret_task(1, 0, 1, 2)
+    x_send_last(6).start()
+    ret_task(1, 0, 2, 1)
+    ret_task(0, 0, 2, 4)
+    ret_task(0, 1, 2, 2)
+    x_send(1, 7).start()
+    x_send(1, 5).start()
+    ret_task(1, 1, 1, 2)
+    z_task(2, 0, 5, 0)
+    ret_task(1, 1, 3, 0)
+    z_task(2, 1, 5, 1)
+    gate_up(1, 1, 1)
+    z_task(2, 1, 5, 0)
+    ret_task(1, 0, 3, 0)
+    z_task(2, 0, 5, 1)
+    cross(0, 4)
+    cross(0, 3)
+    gate_up(1, 2, 0)
+    ret_task(1, 1, 3, 1)
+    ret_task(1, 0, 2, 2)
+    gate_up(1, 2, 1)
+    gate_up(1, 2, 2)
+    gate_up(1, 2, 3)
+    ret_task(1, 1, 2, 2)
+    ret_task(1, 0, 3, 1)
+    cross(0, 2)
     hidden(1, 0)
-    ret(1, 1, 0, 1)
-    cross(0, 3, 4)
-    z_step(2, 5)
-    ret(1, 1, 2)
-    ret(1, 2, 0, 1)
-    gate_up(1, 1)
-    ret(1, 2, 2)
-    ret(1, 3, 0, 1)
-    gate_up(1, 2)
+    ret_task(1, 0, 4, 0)
+    ret_task(0, 0, 1, 2)
+    hidden(1, 2)
+    ret_task(0, 1, 2, 4)
+    ret_task(1, 1, 4, 0)
+    ret_task(1, 1, 4, 1)
+    gate_up(1, 1, 2)
+    gate_up(1, 1, 3)
+    ret_task(1, 0, 4, 1)
+    down(1, 2, 'b')
+    down(1, 2, 'a')
+    ret_task(2, 0, 1, 0)
+    cross(1, 7)
     hidden(1, 1)
-    cross(0, 1, 2)
-    hidden(1, 2)
-    down(1, 0)
-    ret(1, 3, 2)
-    ret(1, 4, 0, 1)
-    down(1, 2)
-    cross(1, 7)
-    ret(2, 1, 0, 1)
+    ret_task(2, 1, 1, 0)
+    ret_task(1, 0, 3, 2)
+    ret_task(2, 1, 1, 1)
+    ret_task(1, 1, 3, 2)
+    ret_task(2, 0, 1, 1)
+    down(1, 1, 'b')
+    down(1, 1, 'a')
+    ret_task(2, 0, 2, 0)
+    cross(1, 6)
+    ret_task(2, 1, 2, 0)
+    ret_task(1, 0, 4, 2)
+    down(1, 0, 'b')
+    ret_task(2, 1, 1, 2)
+    cross(1, 5)
+    ret_task(2, 0, 1, 2)
+    finish(1, 0)
     cross(0, 0)
-    down(1, 1)
-    cross(1, 5, 6)
-    ret(1, 4, 2)
-    ret(2, 2, 0, 1)
-    ret(2, 1, 3, 2)
-    finish(1, 0, 1)
-    cross(1, 3, 4)
-    ret(0, 1, 4)
-    ret(2, 3, 0, 1)
-    ret(2, 2, 3, 2)
-    ret(0, 1, 2)
-    ret(0, 2, 4)
+    ret_task(2, 1, 2, 1)
+    cross(1, 4)
+    ret_task(2, 0, 1, 3)
+    down(1, 0, 'a')
+    ret_task(2, 0, 3, 0)
+    ret_task(2, 1, 3, 0)
+    ret_task(2, 1, 2, 2)
+    ret_task(2, 0, 2, 1)
+    ret_task(2, 1, 3, 1)
+    cross(1, 2)
+    cross(1, 3)
+    ret_task(2, 0, 2, 2)
+    ret_task(2, 0, 3, 1)
+    ret_task(1, 1, 4, 2)
+    finish(1, 1)
+    ret_task(2, 1, 2, 3)
+    ret_task(2, 0, 4, 0)
+    ret_task(2, 1, 4, 0)
+    ret_task(2, 0, 2, 3)
+    ret_task(2, 0, 4, 1)
+    cross(1, 1)
+    ret_task(2, 1, 3, 3)
+    ret_task(2, 1, 4, 1)
+    ret_task(2, 1, 3, 2)
+    cross(1, 0)
+    ret_task(2, 0, 3, 3)
+    ret_task(2, 0, 3, 2)
     finish(1, 2)
-    cross(1, 1, 2, 0)
+    finish(2, 0)
+    ret_task(2, 1, 4, 3)
     hand_out(1, 0)
+    finish(2, 1)
+    ret_task(2, 0, 4, 3)
+    ret_task(0, 0, 3, 4)
+    ret_task(0, 1, 3, 4)
+    ret_task(0, 0, 2, 2)
     hand_out(1, 1)
-    ret(2, 4, 0, 1)
-    ret(2, 3, 3, 2)
-    ret(0, 2, 2)
-    ret(0, 3, 4)
-    finish(2, 0, 1)
-    ret(2, 4, 3, 2)
-    ret(0, 3, 2)
-    ret(0, 4, 4)
+    ret_task(0, 1, 3, 2)
+    ret_task(2, 1, 4, 2)
+    ret_task(2, 0, 4, 2)
+    finish(2, 3)
     hand_out(2, 0)
-    finish(2, 3)
+    ret_task(0, 0, 4, 4)
+    ret_task(0, 0, 3, 2)
+    ret_task(0, 1, 4, 4)
+    hand_out_last()
     finish(2, 2)
     hand_out(2, 1)
-    ret(0, 4, 2)
-    hand_out_last()
-    finish(0, 4, 2)
+    ret_task(0, 0, 4, 2)
+    ret_task(0, 1, 4, 2)
+    finish(0, 4)
     hand_out(0, 0)
+    finish(0, 2)
     hand_out(0, 1)
+
     seven = pl.ds(0, 7)
     wait_for(as_sem.at[0], send.at[seven])
     wait_for(as_sem.at[1], send_x.at[seven])
@@ -593,12 +758,15 @@
     for sem in (xs_sem, ys_sem):
         wait_for(sem.at[2], yxo)
     gate_col = jnp.sum(jnp.where(rows_i == cols_i, gate_ref[...], 0.0), axis=1, keepdims=True)
+    halves = ((0, result_a, 0, wa), (1, result_b, wa, wa + wb))
+    rows = []
+    for kind, result, lo, hi in halves:
+        wait_for(dr_sem.at[kind], result.at[seven])
+        rows.append(dot(sel[0], result[...].reshape(EXPERTS * MAIN, hi - lo)))
     wait_for(dr_sem.at[2], result_x.at[seven])
     extra = unfold([result_x[...].reshape(EXPERTS * MAIN, 128)], (wa + wb) // 128)
-    for kind, result, lo, hi in ((0, result_a, 0, wa), (1, result_b, wa, wa + wb)):
-        wait_for(dr_sem.at[kind], result.at[seven])
-        rows = dot(sel[0], result[...].reshape(EXPERTS * MAIN, hi - lo)) + dot(sel[1][:, :16], extra[:, lo:hi])
-        out_ref[:, lo:hi] = (gate_col * rows).astype(BF16)
+    for kind, _, lo, hi in halves:
+        out_ref[:, lo:hi] = (gate_col * (rows[kind] + dot(sel[1][:, :16], extra[:, lo:hi]))).astype(BF16)
     for kind, parcel in enumerate((parcel_a, parcel_b, parcel_x)):
         wait_for(ds_sem.at[kind], parcel.at[seven])
 

time: 129 us -> 119 us (0.922)
  Pallas kernels: 127 us -> 117 us
    pallas_call x1, Pallas kernels: 127 us -> 117 us  [local(): pl.pallas_call(kernel, out_shape=jax.ShapeDtypeStruct((n_tok, wa + wb), B...]
where the time goes in v7:
time: 119 us
  Pallas kernels  117 us (98%)
  local copies, waits for them, and re-layouts  1.77 us (1%)
    pallas_call x1, Pallas kernels, local(): pl.pallas_call(kernel, out_shape=jax.ShapeDtypeStruct((n_tok, wa + wb), B...  117 us

profile of v7, /device:TPU:6, one launch (start us, length us, event | category | flops | bytes accessed | tf_op | source)
XLA Modules:
  0.0 119.1 jit_solution(14747066421257797400)
XLA Ops:
  0.0 117.3 %routed_experts.1 = bf16[128,1536]{1,0:T(8,128)(2,1)} custom-call(bf16[128,6144]{1,0:T(8,128)(2,1)} %tok_ref.1, s32[1,128]{1,0:T(1,128)} %bitcast.2, f32[1,128]{1,0:T(1,128)} %bitcast.3, bf16[168,6144]{1,0:T(8,128)(2,1)} %wg_ref.1, bf16[168,6144]{1,0:T(8,128)(2,1)} %wu_ref.1, bf16[168,6144]{1,0:T(8,128)(2,1)} %wd_ref.1), custom_call_target="tpu_custom_call" | custom-call | flops 7000000000 | bytes 10000000 | tf_op jit(solution)/shard_map/routed_experts/pallas_call | solution.py:789
  117.3 1.8 %copy.8 = bf16[128,1536]{1,0:T(8,128)(2,1)} copy(bf16[128,1536]{1,0:T(8,128)(2,1)} %routed_experts.1) | data formatting | bytes 786432
